TPU v7x, 512 devices: a whole 4x4x16 slice. The times are simulated.
512 devices in a mesh: chaos: 32 (over y, x, core), sx: 4 (over z_hi), sy: 4 (over z_lo).
Axes of the slice: x: 4, y: 4, z: 16 (z_hi: 4, z_lo: 4; z = z_hi * 4 + z_lo), core: 2. Of those that a mesh axis runs over, the one named last changes fastest.
Arguments:
- right_side: float32 [512, 128, 512], P('chaos', 'sx', 'sy'), may hold values from -6 to 6
- mean_coef: float32 [128, 512], P('sx', 'sy'), may hold values from 0.2 to 2
- mode_coef: float32 [10, 128, 512], P(None, 'sx', 'sy'), may hold values from -0.6 to 0.6
- coupling: bfloat16 [10, 2, 8, 4096], replicated, may hold values from -0.375 to 0.375
- offsets: int32 [10, 2], replicated, may hold values from 0 to 7
- lower_bound: float32 [1], replicated, may hold values from 0.5 to 3
- upper_bound: float32 [1], replicated, may hold values from 10 to 30
Outputs:
- solution: float32 [512, 128, 512], P('chaos', 'sx', 'sy')
Inputs may be any that keep to these rules, and one draw needn't show every extreme that they name: Block diagonal offsets; a mode may repeat an offset, and repeated diagonals add.
All inputs are finite; a program needn't handle non-finite values.
Results may differ from a plain program's by a relative error of at most 0.0003.
Values sent between devices are 32-bit elements; how exact they have to be, the bound alone decides.
No kernel may reach another device: no remote copies, remote signals or barrier semaphores. Data moves between devices by JAX's collectives and lax.ppermute only.
A program may use at most 64 MiB of HBM per device.

v0:
```python
import math

import jax
import jax.numpy as jnp
from jax import lax
from jax.sharding import PartitionSpec as P

highest = lax.Precision.HIGHEST


def extended(cells, sides, width):
    for axis, dim in sides:
        count = lax.axis_size(axis)
        head = lax.slice_in_dim(cells, 0, width, axis=dim)
        tail = lax.slice_in_dim(cells, cells.shape[dim] - width, cells.shape[dim], axis=dim)
        cells = jnp.concatenate(
            [
                lax.ppermute(tail, axis, [(i, (i + 1) % count) for i in range(count)]),
                cells,
                lax.ppermute(head, axis, [((i + 1) % count, i) for i in range(count)]),
            ],
            axis=dim,
        )
    return cells


def plane_view(values):
    return values.reshape(values.shape[:-1] + (values.shape[-1] // 2, 2))


def faces_of(padded):
    center = padded[..., 1:-1, 1:-1, :]
    others = [
        padded[..., :-2, 1:-1, :],
        padded[..., 2:, 1:-1, :],
        padded[..., 1:-1, :-2, :],
        padded[..., 1:-1, 2:, :],
        center[..., ::-1],
    ]
    return (center, others)


def mix_terms(moved, coupling, offsets):
    mode_count, term_count, width = moved.shape
    diag_count = offsets.shape[1]
    block_count = coupling.shape[2]
    block_size = math.isqrt(coupling.shape[3])
    blocks = moved.reshape(mode_count, block_count, block_size, width)
    mixed = jnp.zeros((block_count, block_size, width), jnp.float32)
    for mode_index in range(mode_count):
        source = blocks[mode_index]
        for diag_index in range(diag_count):
            shift_by = offsets[mode_index, diag_index]
            matrix = coupling[mode_index, diag_index].reshape(block_count, block_size, block_size)
            matrix = matrix.astype(jnp.float32)
            mixed = mixed + jnp.einsum(
                "dab,dbc->dac", matrix, jnp.roll(source, -shift_by, axis=0), precision=highest
            )
            mixed = mixed + jnp.roll(
                jnp.einsum("dba,dbc->dac", matrix, source, precision=highest), shift_by, axis=0
            )
    return mixed.reshape(term_count, width)


def per_device(right_side, mean_coef, mode_coef, coupling, offsets, lower_bound, upper_bound):
    chaos_count = lax.axis_size("chaos")
    local_terms, tile_rows, tile_width = right_side.shape
    own_rows = tile_rows // chaos_count
    mode_count = mode_coef.shape[0]
    all_terms = local_terms * chaos_count
    coefficients = plane_view(jnp.concatenate([mean_coef[None], mode_coef], axis=0))
    padded_coef = extended(coefficients, (("sx", 1), ("sy", 2)), 1)
    center, beside = faces_of(padded_coef)
    weights = jnp.stack([(center + other) * 0.5 for other in beside], axis=1)
    lower_end = lower_bound[0]
    upper_end = upper_bound[0]
    middle_value = (upper_end + lower_end) * 0.5
    half_width = (upper_end - lower_end) * 0.5
    spread_ratio = middle_value / half_width
    factor_now = 1.0 / spread_ratio
    direction = right_side / middle_value
    solution = direction
    residual = right_side
    view = plane_view(direction)
    padded = extended(view, (("sx", 1), ("sy", 2)), 1)
    middle, beside_all = faces_of(padded)
    differences = jnp.stack([middle - other for other in beside_all], axis=0)
    result = view
    for face in range(5):
        result = result + weights[0, face][None] * differences[face]
    diffused = weights[1:, 0][:, None] * differences[0][None]
    for face in range(1, 5):
        diffused = diffused + weights[1:, face][:, None] * differences[face][None]
    moved = lax.all_to_all(
        diffused.reshape(mode_count, local_terms, tile_rows, tile_width),
        "chaos",
        split_axis=2,
        concat_axis=1,
        tiled=True,
    )
    mixed = mix_terms(
        moved.reshape(mode_count, all_terms, own_rows * tile_width), coupling, offsets
    )
    returned = lax.all_to_all(
        mixed.reshape(all_terms, own_rows, tile_width),
        "chaos",
        split_axis=0,
        concat_axis=1,
        tiled=True,
    )
    residual = residual - (result.reshape(direction.shape) + returned)
    factor_next = 1.0 / (2.0 * spread_ratio - factor_now)
    direction = factor_next * factor_now * direction + 2.0 * factor_next / half_width * residual
    solution = solution + direction
    return solution


def solution(mesh):
    return jax.shard_map(
        per_device,
        mesh=mesh,
        in_specs=(P("chaos", "sx", "sy"), P("sx", "sy"), P(None, "sx", "sy"), P(), P(), P(), P()),
        out_specs=P("chaos", "sx", "sy"),
        check_vma=False,
    )
```

profile of v0, /device:TPU:1, one launch (start us, length us, event | category | flops | bytes accessed | tf_op | source)
XLA Modules:
  0.0 220.3 jit_solution(17091357869322692856)
XLA Ops:
  0.0 1.2 copy.120
  2.0 1.1 fusion.43
  3.4 13.3 %collective-permute-start.2 = (f32[11,1,64,2]{2,3,1,0:T(2,128)S(1)}, f32[11,1,64,2]{2,3,1,0:T(2,128)}, u32[]{:S(2)}, u32[]{:S(2)}) collective-permute-start(f32[11,1,64,2]{2,3,1,0:T(2,128)S(1)} %copy.125), channel_id=1, source_target_pairs={{4,0},{8,4},{12,8},{0,12},{5,1},{9,5},{13,9},{1,13},{6,2},{10,6},{... | collective-permute-start | bytes 16904 | tf_op jit(solution)/shard_map/ppermute | solution.py:20
  17.6 1.9 collective-permute-start
  21.4 1.4 fusion.161
  22.8 1.8 copy.123
  24.5 5.2 %collective-permute-start.1 = (f32[16,1,64,2]{2,0,3,1:T(8,128)S(1)}, f32[16,1,64,2]{2,0,3,1:T(8,128)}, u32[]{:S(2)}, u32[]{:S(2)}) collective-permute-start(f32[16,1,64,2]{2,0,3,1:T(8,128)S(1)} %copy.123), channel_id=1, source_target_pairs={{0,4},{4,8},{8,12},{12,0},{1,5},{5,9},{9,13},{13,1},{2,6},{6,10},{... | collective-permute-start | bytes 24584 | tf_op jit(solution)/shard_map/ppermute | solution.py:18
  29.7 1.2 copy.127
  30.9 4.0 %collective-permute-start.3 = (f32[16,1,64,2]{2,0,3,1:T(8,128)}, f32[16,1,64,2]{2,0,3,1:T(8,128)}, u32[]{:S(2)}, u32[]{:S(2)}) collective-permute-start(f32[16,1,64,2]{2,0,3,1:T(8,128)} %copy.127), channel_id=1, source_target_pairs={{4,0},{8,4},{12,8},{0,12},{5,1},{9,5},{13,9},{1,13},{6,2},{10,6},{... | collective-permute-start | bytes 24584 | tf_op jit(solution)/shard_map/ppermute | solution.py:20
  35.3 3.3 %rev.6 = f32[11,32,64,2]{1,3,2,0:T(2,128)} reverse(f32[11,32,64,2]{1,3,2,0:T(2,128)S(1)} %pad_maximum_fusion.8), dimensions={3} | reverse | bytes 360448 | tf_op jit(solution)/shard_map/rev | solution.py:38
  38.6 1.1 copy.126
  39.7 2.7 %fusion.50 = (f32[11,32,64,2]{1,3,2,0:T(2,128)S(1)}, f32[11,32,64,2]{1,3,2,0:T(2,128)S(1)}) fusion(f32[11,1,64,2]{1,3,2,0:T(2,128)S(1)} %copy.126, f32[10,32,64,2]{1,3,2,0:T(2,128)S(1)} %bitcast.339, f32[1,32,64,2]{1,3,2,0:T(2,128)S(1)} %bitcast.396, f32[11,32,64,2]{1,3,2,0:T(2,128)} %rev.6), kind=kLoop, calls=%fused_computation.113 | loop fusion | flops 315392 | bytes 726528 | tf_op jit(solution)/shard_map/mul | solution.py:74
  43.6 1.1 copy.122
  46.0 0.9 slice.344
  46.9 0.9 slice.347
  47.8 2.6 %collective-permute-start.4 = (f32[11,34,1,2]{1,3,2,0:T(2,128)}, f32[11,34,1,2]{1,3,2,0:T(2,128)}, u32[]{:S(2)}, u32[]{:S(2)}) collective-permute-start(f32[11,34,1,2]{1,3,2,0:T(2,128)} %get-tuple-element.23), channel_id=1, source_target_pairs={{0,1},{1,2},{2,3},{3,0},{4,5},{5,6},{6,7},{7,4},{8,9},{9,10},{10,1... | collective-permute-start | bytes 8984 | tf_op jit(solution)/shard_map/ppermute | solution.py:18
  50.5 4.4 %collective-permute-start.6 = (f32[11,34,1,2]{1,3,2,0:T(2,128)}, f32[11,34,1,2]{1,3,2,0:T(2,128)}, u32[]{:S(2)}, u32[]{:S(2)}) collective-permute-start(f32[11,34,1,2]{1,3,2,0:T(2,128)} %get-tuple-element.24), channel_id=1, source_target_pairs={{1,0},{2,1},{3,2},{0,3},{5,4},{6,5},{7,6},{4,7},{9,8},{10,9},{11,1... | collective-permute-start | bytes 8984 | tf_op jit(solution)/shard_map/ppermute | solution.py:20
  54.9 2.1 copy.135
  57.0 2.1 copy.141
  59.1 1.7 copy.124
  60.8 2.6 %copy.128 = f32[16,1,64,2]{1,0,3,2:T(8,128)} copy(f32[16,1,64,2]{2,0,3,1:T(8,128)} %collective-permute-done.3) | data formatting | bytes 16384 | tf_op jit(solution)/shard_map/ppermute | solution.py:20
  63.4 3.8 %fusion.42 = (f32[16,32,64,2]{1,0,3,2:T(8,128)}, f32[16,32,64,2]{1,0,3,2:T(8,128)}, f32[16,32,64,2]{1,0,3,2:T(8,128)}) fusion(f32[16,32,64,2]{1,0,3,2:T(8,128)S(1)} %bitcast.334, f32[16,1,64,2]{1,0,3,2:T(8,128)S(1)} %copy.124, f32[16,1,64,2]{1,0,3,2:T(8,128)} %copy.128), kind=kLoop, calls=%fused_computation.92 | loop fusion | flops 327680 | bytes 1064960 | tf_op jit(solution)/shard_map/sub | solution.py:87
  67.9 1.9 collective-permute-start.5
  69.8 5.3 %collective-permute-start.7 = (f32[16,34,1,2]{1,0,3,2:T(8,128)}, f32[16,34,1,2]{1,0,3,2:T(8,128)}, u32[]{:S(2)}, u32[]{:S(2)}) collective-permute-start(f32[16,34,1,2]{1,0,3,2:T(8,128)} %get-tuple-element.9), channel_id=1, source_target_pairs={{1,0},{2,1},{3,2},{0,3},{5,4},{6,5},{7,6},{4,7},{9,8},{10,9},{11,1... | collective-permute-start | bytes 13064 | tf_op jit(solution)/shard_map/ppermute | solution.py:20
  75.1 2.4 %copy.134 = f32[16,32,128]{2,0,1:T(8,128)} copy(f32[16,32,128]{1,0,2:T(8,128)} %bitcast.388) | data formatting | bytes 524288 | tf_op jit(solution)/shard_map/mul | solution.py:91
  77.5 2.4 %copy.136 = f32[16,32,128]{2,0,1:T(8,128)} copy(f32[16,32,128]{1,0,2:T(8,128)} %bitcast.387) | data formatting | bytes 524288 | tf_op jit(solution)/shard_map/mul | solution.py:93
  79.8 2.4 %copy.142 = f32[16,32,128]{2,0,1:T(8,128)} copy(f32[16,32,128]{1,0,2:T(8,128)} %bitcast.386) | data formatting | bytes 524288 | tf_op jit(solution)/shard_map/mul | solution.py:93
  82.2 6.2 %fusion.48 = (f32[11,32,64,2]{1,3,2,0:T(2,128)S(1)}, f32[11,32,64,2]{1,3,2,0:T(2,128)S(1)}, f32[11,32,64,2]{1,3,2,0:T(2,128)S(1)}) fusion(f32[11,34,1,2]{1,3,2,0:T(2,128)} %collective-permute-done.4, f32[11,1,64,2]{1,3,2,0:T(2,128)S(1)} %copy.126, f32[11,1,64,2]{1,3,2,0:T(2,128)} %copy-done.1, f32[10,32,64,2]{1,3,2,0:T(2,128)S(1)} %bitcast.341, ...), kind=kLoop, calls=%fused_computation.107 | loop fusion | flops 765952 | bytes 738144 | tf_op jit(solution)/shard_map/mul | solution.py:74
  89.2 0.9 slice.346
  90.1 1.0 copy.133
  91.2 1.0 copy.137
  92.2 1.4 copy.139
  93.6 5.2 %multiply_add_fusion.1 = (f32[16,32,64,2]{1,0,3,2:T(8,128)}, f32[16,32,64,2]{1,0,3,2:T(8,128)}, f32[16,32,64,2]{1,0,3,2:T(8,128)}) fusion(f32[16,32,64,2]{1,0,3,2:T(8,128)S(1)} %bitcast.336, f32[32,64,2]{0,2,1:T(2,128)S(1)} %copy-done.29, f32[32,64,2]{0,2,1:T(2,128)} %get-tuple-element.75, f32[32,64,2]{0,2,1:T(2,128)} %get-tuple-element.76, ...), kind=kLoop, calls=%fused_computation.93 | loop fusion | flops 1507328 | bytes 1155584 | tf_op jit(solution)/shard_map/add | solution.py:90
  98.9 1.8 copy.138
  100.7 1.7 copy.140
  102.5 2.8 %multiply_add_fusion = f32[10,16,32,128]{3,1,0,2:T(8,128)} fusion(f32[16,32,128]{2,0,1:T(8,128)S(1)} %copy-done.24, f32[10,32,128]{2,0,1:T(8,128)S(1)} %copy-done.21, f32[16,32,128]{2,0,1:T(8,128)S(1)} %copy.140, f32[10,32,128]{2,0,1:T(8,128)S(1)} %copy.139, f32[16,32,128]{2,0,1:T(8,128)S(1)} %copy.138, f32[10,32,128]{2,0,1:T(8,128)S(1)} %copy-done.26, ...), kind=kLoop, calls=%fused_computation | loop fusion | flops 5898240 | bytes 4751360 | tf_op jit(solution)/shard_map/add | solution.py:93
  105.3 10.1 %all-to-all-start = ((f32[10,16,32,128]{3,1,0,2:T(8,128)}), f32[10,16,32,128]{3,1,0,2:T(8,128)S(1)}, u32[]{:S(2)}, u32[]{:S(2)}) async-start(f32[10,16,32,128]{3,1,0,2:T(8,128)} %multiply_add_fusion), calls=%async_computation | async-start | bytes 5242880 | tf_op jit(solution)/shard_map/all_to_all | solution.py:94
  167.1 1.5 slice.329
  168.6 2.1 fusion.160
  172.3 1.0 reshape_squeeze.60
  173.4 1.7 reshape_squeeze.63
  175.1 1.7 reshape_squeeze.64
  176.7 1.7 reshape_squeeze.65
  185.9 1.0 reshape_squeeze.78
  186.9 1.0 reshape_squeeze.79
  202.2 1.0 fusion.1
  203.2 7.4 %all-to-all-start.1 = ((f32[512,1,128]{2,1,0:T(1,128)}), f32[512,1,128]{2,1,0:T(1,128)S(1)}, u32[]{:S(2)}, u32[]{:S(2)}) async-start(f32[512,1,128]{2,1,0:T(1,128)} %bitcast.95), calls=%async_computation.1 | async-start | bytes 524288 | tf_op jit(solution)/shard_map/all_to_all | solution.py:104
  211.2 8.3 %all-to-all-done.1 = f32[512,1,128]{2,1,0:T(1,128)S(1)} async-done(((f32[512,1,128]{2,1,0:T(1,128)}), f32[512,1,128]{2,1,0:T(1,128)S(1)}, u32[]{:S(2)}, u32[]{:S(2)}) %all-to-all-start.1) | async-done | bytes 262176 | tf_op jit(solution)/shard_map/all_to_all | solution.py:104
  (142 shorter events, 32.0 us)
Async XLA Ops:
  0.0 20.8 %copy-start.27 = (f32[16,32,128]{2,1,0:T(8,128)S(1)}, f32[16,32,128]{2,1,0:T(8,128)}, u32[]{:S(2)}) copy-start(f32[16,32,128]{2,1,0:T(8,128)} %param.9) | copy-start | bytes 786436
  3.4 35.2 %collective-permute-start.2 = (f32[11,1,64,2]{2,3,1,0:T(2,128)S(1)}, f32[11,1,64,2]{2,3,1,0:T(2,128)}, u32[]{:S(2)}, u32[]{:S(2)}) collective-permute-start(f32[11,1,64,2]{2,3,1,0:T(2,128)S(1)} %copy.125), channel_id=1, source_target_pairs={{4,0},{8,4},{12,8},{0,12},{5,1},{9,5},{13,9},{1,13},{6,2},{10,6},{... | collective-permute-start | bytes 16904 | tf_op jit(solution)/shard_map/ppermute | solution.py:20
  17.6 25.9 %collective-permute-start = (f32[11,1,64,2]{2,3,1,0:T(2,128)}, f32[11,1,64,2]{2,3,1,0:T(2,128)}, u32[]{:S(2)}, u32[]{:S(2)}) collective-permute-start(f32[11,1,64,2]{2,3,1,0:T(2,128)} %copy.121), channel_id=1, source_target_pairs={{0,4},{4,8},{8,12},{12,0},{1,5},{5,9},{9,13},{13,1},{2,6},{6,10},{... | collective-permute-start | bytes 16904 | tf_op jit(solution)/shard_map/ppermute | solution.py:18
  24.5 34.6 %collective-permute-start.1 = (f32[16,1,64,2]{2,0,3,1:T(8,128)S(1)}, f32[16,1,64,2]{2,0,3,1:T(8,128)}, u32[]{:S(2)}, u32[]{:S(2)}) collective-permute-start(f32[16,1,64,2]{2,0,3,1:T(8,128)S(1)} %copy.123), channel_id=1, source_target_pairs={{0,4},{4,8},{8,12},{12,0},{1,5},{5,9},{9,13},{13,1},{2,6},{6,10},{... | collective-permute-start | bytes 24584 | tf_op jit(solution)/shard_map/ppermute | solution.py:18
  30.9 29.9 %collective-permute-start.3 = (f32[16,1,64,2]{2,0,3,1:T(8,128)}, f32[16,1,64,2]{2,0,3,1:T(8,128)}, u32[]{:S(2)}, u32[]{:S(2)}) collective-permute-start(f32[16,1,64,2]{2,0,3,1:T(8,128)} %copy.127), channel_id=1, source_target_pairs={{4,0},{8,4},{12,8},{0,12},{5,1},{9,5},{13,9},{1,13},{6,2},{10,6},{... | collective-permute-start | bytes 24584 | tf_op jit(solution)/shard_map/ppermute | solution.py:20
  42.4 0.9 copy-start.3
  42.4 1.2 copy-start.5
  44.6 14.5 %copy-start.1 = (f32[11,1,64,2]{1,3,2,0:T(2,128)}, f32[11,1,64,2]{1,3,2,0:T(2,128)S(1)}, u32[]{:S(2)}) copy-start(f32[11,1,64,2]{1,3,2,0:T(2,128)S(1)} %copy.122) | copy-start | bytes 16900
  44.6 1.4 copy-start.6
  44.6 2.3 %copy-start.4 = (f32[11,32,64,2]{1,3,2,0:T(2,128)S(1)}, f32[11,32,64,2]{1,3,2,0:T(2,128)}, u32[]{:S(2)}) copy-start(f32[11,32,64,2]{1,3,2,0:T(2,128)} %copy-done.3) | copy-start | bytes 540676
  47.8 34.4 %collective-permute-start.4 = (f32[11,34,1,2]{1,3,2,0:T(2,128)}, f32[11,34,1,2]{1,3,2,0:T(2,128)}, u32[]{:S(2)}, u32[]{:S(2)}) collective-permute-start(f32[11,34,1,2]{1,3,2,0:T(2,128)} %get-tuple-element.23), channel_id=1, source_target_pairs={{0,1},{1,2},{2,3},{3,0},{4,5},{5,6},{6,7},{7,4},{8,9},{9,10},{10,1... | collective-permute-start | bytes 8984 | tf_op jit(solution)/shard_map/ppermute | solution.py:18
  50.5 31.8 %collective-permute-start.6 = (f32[11,34,1,2]{1,3,2,0:T(2,128)}, f32[11,34,1,2]{1,3,2,0:T(2,128)}, u32[]{:S(2)}, u32[]{:S(2)}) collective-permute-start(f32[11,34,1,2]{1,3,2,0:T(2,128)} %get-tuple-element.24), channel_id=1, source_target_pairs={{1,0},{2,1},{3,2},{0,3},{5,4},{6,5},{7,6},{4,7},{9,8},{10,9},{11,1... | collective-permute-start | bytes 8984 | tf_op jit(solution)/shard_map/ppermute | solution.py:20
  63.4 3.8 %copy-start = (f32[16,1,64,2]{1,0,3,2:T(8,128)S(1)}, f32[16,1,64,2]{1,0,3,2:T(8,128)}, u32[]{:S(2)}) copy-start(f32[16,1,64,2]{1,0,3,2:T(8,128)} %copy.128) | copy-start | bytes 24580
  67.9 25.8 %collective-permute-start.5 = (f32[16,34,1,2]{1,0,3,2:T(8,128)}, f32[16,34,1,2]{1,0,3,2:T(8,128)S(1)}, u32[]{:S(2)}, u32[]{:S(2)}) collective-permute-start(f32[16,34,1,2]{1,0,3,2:T(8,128)} %get-tuple-element.10), channel_id=1, source_target_pairs={{0,1},{1,2},{2,3},{3,0},{4,5},{5,6},{6,7},{7,4},{8,9},{9,10},{10,1... | collective-permute-start | bytes 13064 | tf_op jit(solution)/shard_map/ppermute | solution.py:18
  69.8 23.9 %collective-permute-start.7 = (f32[16,34,1,2]{1,0,3,2:T(8,128)}, f32[16,34,1,2]{1,0,3,2:T(8,128)}, u32[]{:S(2)}, u32[]{:S(2)}) collective-permute-start(f32[16,34,1,2]{1,0,3,2:T(8,128)} %get-tuple-element.9), channel_id=1, source_target_pairs={{1,0},{2,1},{3,2},{0,3},{5,4},{6,5},{7,6},{4,7},{9,8},{10,9},{11,1... | collective-permute-start | bytes 13064 | tf_op jit(solution)/shard_map/ppermute | solution.py:20
  89.2 4.5 %copy-start.29 = (f32[32,64,2]{0,2,1:T(2,128)S(1)}, f32[32,64,2]{0,2,1:T(2,128)}, u32[]{:S(2)}) copy-start(f32[32,64,2]{0,2,1:T(2,128)} %get-tuple-element.73) | copy-start | bytes 49156
  98.9 3.5 %copy-start.20 = (f32[10,32,128]{2,0,1:T(8,128)S(1)}, f32[10,32,128]{2,0,1:T(8,128)}, u32[]{:S(2)}) copy-start(f32[10,32,128]{2,0,1:T(8,128)} %copy.135) | copy-start | bytes 491524
  98.9 3.5 %copy-start.21 = (f32[10,32,128]{2,0,1:T(8,128)S(1)}, f32[10,32,128]{2,0,1:T(8,128)}, u32[]{:S(2)}) copy-start(f32[10,32,128]{2,0,1:T(8,128)} %copy.141) | copy-start | bytes 491524
  98.9 3.5 %copy-start.22 = (f32[16,32,128]{2,0,1:T(8,128)S(1)}, f32[16,32,128]{2,0,1:T(8,128)}, u32[]{:S(2)}) copy-start(f32[16,32,128]{2,0,1:T(8,128)} %copy.134) | copy-start | bytes 786436
  98.9 3.5 %copy-start.23 = (f32[16,32,128]{2,0,1:T(8,128)S(1)}, f32[16,32,128]{2,0,1:T(8,128)}, u32[]{:S(2)}) copy-start(f32[16,32,128]{2,0,1:T(8,128)} %copy.136) | copy-start | bytes 786436
  98.9 3.5 %copy-start.24 = (f32[16,32,128]{2,0,1:T(8,128)S(1)}, f32[16,32,128]{2,0,1:T(8,128)}, u32[]{:S(2)}) copy-start(f32[16,32,128]{2,0,1:T(8,128)} %copy.142) | copy-start | bytes 786436
  98.9 3.5 %copy-start.25 = (f32[10,32,128]{2,0,1:T(8,128)S(1)}, f32[10,32,128]{2,0,1:T(8,128)}, u32[]{:S(2)}) copy-start(f32[10,32,128]{2,0,1:T(8,128)} %copy.133) | copy-start | bytes 491524
  98.9 3.5 %copy-start.26 = (f32[10,32,128]{2,0,1:T(8,128)S(1)}, f32[10,32,128]{2,0,1:T(8,128)}, u32[]{:S(2)}) copy-start(f32[10,32,128]{2,0,1:T(8,128)} %copy.137) | copy-start | bytes 491524
  105.3 10.1 %copy-start.30 = (s32[10,2]{0,1:T(2,128)S(1)}, s32[10,2]{0,1:T(2,128)}, u32[]{:S(2)}) copy-start(s32[10,2]{0,1:T(2,128)} %param.13) | copy-start | bytes 244
  105.3 83.0 %all-to-all-start = ((f32[10,16,32,128]{3,1,0,2:T(8,128)}), f32[10,16,32,128]{3,1,0,2:T(8,128)S(1)}, u32[]{:S(2)}, u32[]{:S(2)}) async-start(f32[10,16,32,128]{3,1,0,2:T(8,128)} %multiply_add_fusion), calls=%async_computation | async-start | bytes 5242880 | tf_op jit(solution)/shard_map/all_to_all | solution.py:94
  188.3 0.9 copy-start.19
  188.3 1.5 copy-start.15
  188.3 1.9 copy-start.18
  188.6 1.9 copy-start.17
  188.6 2.2 %copy-start.16 = (bf16[8,64,64]{2,1,0:T(8,128)(2,1)S(1)}, bf16[8,64,64]{2,1,0:T(8,128)(2,1)}, u32[]{:S(2)}) copy-start(bf16[8,64,64]{2,1,0:T(8,128)(2,1)} %reshape_squeeze.65) | copy-start | bytes 196612
  188.6 2.6 %copy-start.14 = (bf16[8,64,64]{2,1,0:T(8,128)(2,1)S(1)}, bf16[8,64,64]{2,1,0:T(8,128)(2,1)}, u32[]{:S(2)}) copy-start(bf16[8,64,64]{2,1,0:T(8,128)(2,1)} %reshape_squeeze.66) | copy-start | bytes 196612
  188.6 2.9 %copy-start.13 = (bf16[8,64,64]{2,1,0:T(8,128)(2,1)S(1)}, bf16[8,64,64]{2,1,0:T(8,128)(2,1)}, u32[]{:S(2)}) copy-start(bf16[8,64,64]{2,1,0:T(8,128)(2,1)} %reshape_squeeze.67) | copy-start | bytes 196612
  189.2 2.6 %copy-start.12 = (bf16[8,64,64]{2,1,0:T(8,128)(2,1)S(1)}, bf16[8,64,64]{2,1,0:T(8,128)(2,1)}, u32[]{:S(2)}) copy-start(bf16[8,64,64]{2,1,0:T(8,128)(2,1)} %reshape_squeeze.68) | copy-start | bytes 196612
  189.5 2.6 %copy-start.11 = (bf16[8,64,64]{2,1,0:T(8,128)(2,1)S(1)}, bf16[8,64,64]{2,1,0:T(8,128)(2,1)}, u32[]{:S(2)}) copy-start(bf16[8,64,64]{2,1,0:T(8,128)(2,1)} %reshape_squeeze.69) | copy-start | bytes 196612
  189.8 2.6 %copy-start.10 = (bf16[8,64,64]{2,1,0:T(8,128)(2,1)S(1)}, bf16[8,64,64]{2,1,0:T(8,128)(2,1)}, u32[]{:S(2)}) copy-start(bf16[8,64,64]{2,1,0:T(8,128)(2,1)} %reshape_squeeze.70) | copy-start | bytes 196612
  190.2 2.6 %copy-start.9 = (bf16[8,64,64]{2,1,0:T(8,128)(2,1)S(1)}, bf16[8,64,64]{2,1,0:T(8,128)(2,1)}, u32[]{:S(2)}) copy-start(bf16[8,64,64]{2,1,0:T(8,128)(2,1)} %reshape_squeeze.71) | copy-start | bytes 196612
  190.5 2.6 %copy-start.8 = (bf16[8,64,64]{2,1,0:T(8,128)(2,1)S(1)}, bf16[8,64,64]{2,1,0:T(8,128)(2,1)}, u32[]{:S(2)}) copy-start(bf16[8,64,64]{2,1,0:T(8,128)(2,1)} %reshape_squeeze.72) | copy-start | bytes 196612
  190.8 2.6 %copy-start.7 = (bf16[8,64,64]{2,1,0:T(8,128)(2,1)S(1)}, bf16[8,64,64]{2,1,0:T(8,128)(2,1)}, u32[]{:S(2)}) copy-start(bf16[8,64,64]{2,1,0:T(8,128)(2,1)} %reshape_squeeze.73) | copy-start | bytes 196612
  201.2 9.6 %copy-start.2 = (f32[16,32,64,2]{1,0,3,2:T(8,128)S(1)}, f32[16,32,64,2]{1,0,3,2:T(8,128)}, u32[]{:S(2)}) copy-start(f32[16,32,64,2]{1,0,3,2:T(8,128)} %get-tuple-element.6) | copy-start | bytes 786436
  201.6 18.0 %copy-start.28 = (f32[16,32,128]{2,1,0:T(8,128)S(1)}, f32[16,32,128]{2,1,0:T(8,128)}, u32[]{:S(2)}) copy-start(f32[16,32,128]{2,1,0:T(8,128)} %param.9) | copy-start | bytes 786436
  203.2 16.3 %all-to-all-start.1 = ((f32[512,1,128]{2,1,0:T(1,128)}), f32[512,1,128]{2,1,0:T(1,128)S(1)}, u32[]{:S(2)}, u32[]{:S(2)}) async-start(f32[512,1,128]{2,1,0:T(1,128)} %bitcast.95), calls=%async_computation.1 | async-start | bytes 524288 | tf_op jit(solution)/shard_map/all_to_all | solution.py:104
where the time goes:
time: 223 us; the launch traced here: 220 us
  local copies, waits for them, and re-layouts  64.6 us (29%)
  starting transfers between devices  56.1 us (25%)
  between operations  53.2 us (24%)
  other arithmetic  24.5 us (11%)
  matrix products  13.6 us (6%)
  waiting for transfers between devices  8.32 us (4%)
    ppermute x4, starting transfers between devices, extended(): lax.ppermute(head, axis, [((i + 1) % count, i) for i in range(count)])  27.1 us
    another operation x20, local copies, waits for them, and re-layouts, mix_terms(): coupling[mode_index, diag_index]  17.2 us
    mul x8, local copies, waits for them, and re-layouts, per_device(): diffused = diffused + weights[1:, face][:, None] * differences[face][None]  14.9 us
    ppermute x4, starting transfers between devices, extended(): lax.ppermute(tail, axis, [(i, (i + 1) % count) for i in range(count)])  11.6 us
    all_to_all x1, starting transfers between devices, per_device(): lax.all_to_all(diffused.reshape(mode_count, local_terms, tile_rows, tile_...  10.1 us
    mul x2, other arithmetic, per_device(): weights = jnp.stack([(center + other) * 0.5 for other in beside], axis=1)  8.92 us
    all_to_all x1, waiting for transfers between devices, per_device(): lax.all_to_all(mixed.reshape(all_terms, own_rows, tile_width), 'chaos', s...  8.3 us
    dot_general x20, matrix products, mix_terms(): jnp.einsum('dab,dbc->dac', matrix, jnp.roll(source, -shift_by, axis=0), p...  7.43 us
  transfers between devices with their start and end apart: 10, of which 1 were waited for; matrix products, arithmetic and copies ran while one was open for 32% of the time, Pallas kernels for 0%

commit v1 on v0

v1 whole, which is shorter than its diff:
```python
import functools

import jax
import jax.numpy as jnp
from jax import lax
from jax.experimental import pallas as pl
from jax.experimental.pallas import tpu as pltpu
from jax.sharding import PartitionSpec as P

f32 = jnp.float32
bf16 = jnp.bfloat16
MODES = 10


def block_device(bi, bj):
    high, core = ((0, 0), (1, 0), (1, 1), (0, 1))[bi]
    low, y = (0, bj) if bj < 4 else (1, 7 - bj)
    return y * 8 + (2 * high + low) * 2 + core


def device_block(index):
    core, x, y = index % 2, (index // 2) % 4, index // 8
    bi = jnp.where(x < 2, 3 * core, 1 + core)
    bj = jnp.where(x % 2 == 0, y, 7 - y)
    return bi, bj


def lanes():
    return lax.broadcasted_iota(jnp.int32, (8, 128), 1)


def roll(value, shift):
    if isinstance(shift, int):
        shift = shift % 128
        if shift == 0:
            return value
    return pltpu.roll(value, shift, 1)


def swap_chunks(rows, lane):
    rows = list(rows)
    for step in (1, 2, 4):
        low = (lane // 16) & step == 0
        for i in range(8):
            if i & step == 0:
                a, b = rows[i], rows[i + step]
                rows[i] = jnp.where(low, a, roll(b, 16 * step))
                rows[i + step] = jnp.where(low, roll(a, -16 * step), b)
    return rows


def pack_kernel(field, slots):
    lane = lanes()
    column = lane % 16
    for bi in range(4):
        blocks, above, below = [], [], []
        for h in range(2):
            terms = slice(8 * h, 8 * h + 8)
            blocks.append(swap_chunks([field[terms, 8 * bi + i, :] for i in range(8)], lane))
            above.append(field[terms, (8 * bi - 1) % 32, :])
            below.append(field[terms, (8 * bi + 8) % 32, :])
        for bj in range(8):
            at = block_device(bi, bj)
            units = []
            for h in range(2):
                slots[at, 8 * h : 8 * h + 8, :] = blocks[h][bj]
                side = jnp.where(column >= 8, blocks[h][(bj - 1) % 8], blocks[h][(bj + 1) % 8])
                units.append(roll(side, 2 + 4 * h))
            row = jnp.where(column < 4, units[0], units[1])
            row = jnp.where(lane % 32 < 8, row, roll(row, -8))
            row = jnp.where(lane % 64 < 16, row, roll(row, -16))
            row = jnp.where(lane < 32, row, roll(row, -32))
            for h in range(2):
                start = 64 + 32 * h
                next_row = roll(below[h], start - 16 * bj)
                row = jnp.where((lane >= start) & (lane < start + 16), next_row, row)
                last_row = roll(above[h], start + 16 - 16 * bj)
                row = jnp.where((lane >= start + 16) & (lane < start + 32), last_row, row)
            slots[at, 16:24, :] = row


def spread_units(row, lane):
    row = jnp.where(lane < 32, row, roll(row, 32))
    row = jnp.where(lane % 64 < 16, row, roll(row, 16))
    return jnp.where(lane % 32 < 8, row, roll(row, 8))


def prepare_kernel(coupling, offsets, mean_coef, mode_coef, weights, coefs, pairs, tile, parts):
    lane = lanes()
    first = lane < 64
    bi, bj = device_block(lax.axis_index("chaos"))
    tile[0] = mean_coef[...]
    tile[1 : MODES + 1] = mode_coef[...]
    tile[MODES + 1 :] = jnp.zeros((15 - MODES, 32, 128), f32)
    for h in range(2):
        terms = slice(8 * h, 8 * h + 8)
        blocks = swap_chunks([tile[terms, 8 * bi + i, :] for i in range(8)], lane)
        for j in range(8):
            parts[j] = blocks[j]
        coefs[8 * h : 8 * h + 8, :] = parts[bj]
        above = tile[terms, lax.rem(8 * bi + 31, 32), :]
        below = tile[terms, lax.rem(8 * bi + 8, 32), :]
        beside = jnp.where(
            lane < 64,
            pltpu.roll(above, lax.rem(128 - 16 * bj, 128), 1),
            pltpu.roll(below, lax.rem(240 - 16 * bj, 128), 1),
        )
        coefs[16 + 8 * h : 24 + 8 * h, :] = beside
        sides = jnp.where(
            lane % 16 < 8, roll(parts[lax.rem(bj + 7, 8)], -14), roll(parts[lax.rem(bj + 1, 8)], 14)
        )
        coefs[32 + 8 * h : 40 + 8 * h, :] = sides
    out_row = lax.broadcasted_iota(jnp.int32, (64, 128), 0)
    out_col = lax.broadcasted_iota(jnp.int32, (64, 128), 1)
    pick = jnp.where(out_col % 64 == out_row, 1.0, 0.0).astype(bf16)
    wide = lax.broadcasted_iota(jnp.int32, (64, 128), 1) < 64

    def one_mode(k, carry):
        for m in range(32):
            both = coupling[pl.ds(pl.multiple_of(16 * k, 16), 16), 128 * m : 128 * m + 128].astype(f32)
            one, two = both[:8], both[8:]
            pairs[pl.ds(2 * m, 8, 64), :] = jnp.where(first, one, roll(two, 64))
            pairs[pl.ds(2 * m + 1, 8, 64), :] = jnp.where(first, roll(one, 64), two)
        shift_one, shift_two = offsets[2 * k], offsets[2 * k + 1]
        for d in range(8):
            weights[d, k, :, 0:128] = pairs[64 * d : 64 * d + 64, :].astype(bf16)
            from_one = lax.rem(d + 8 - shift_one, 8)
            from_two = lax.rem(d + 8 - shift_two, 8)
            one = pairs[pl.ds(pl.multiple_of(64 * from_one, 64), 64), :]
            two = pairs[pl.ds(pl.multiple_of(64 * from_two, 64), 64), :]
            stack = jnp.concatenate([jnp.where(wide, one, 0.0), jnp.where(wide, 0.0, two)], axis=0)
            turned = lax.dot_general(
                pick, stack.astype(bf16), (((1,), (1,)), ((), ())), preferred_element_type=f32
            )
            weights[d, k, :, 128:256] = turned.astype(bf16)
        return carry

    lax.fori_loop(0, MODES, one_mode, 0)


def edges_kernel(slots, coefs, rows_out, columns_out):
    lane = lanes()
    bi, bj = device_block(lax.axis_index("chaos"))
    row_shift = jnp.where(bi == 0, 0, 16)
    column_shift = jnp.where(bj == 0, 0, 114)
    for r in range(8):
        row = jnp.zeros((8, 128), f32)
        column = jnp.zeros((8, 128), f32)
        for q in range(8):
            at, h = 4 * q + r // 2, r % 2
            block = slots[at, 8 * h : 8 * h + 8, :]
            row = jnp.where(lane // 16 == q, pltpu.roll(block, lax.rem(row_shift + 16 * q, 128), 1), row)
            column = jnp.where(
                (lane % 16) // 2 == q, pltpu.roll(block, lax.rem(column_shift + 2 * q, 128), 1), column
            )
        rows_out[8 * r : 8 * r + 8, :] = row
        columns_out[8 * r : 8 * r + 8, :] = column
    rows_out[64:80, :] = coefs[0:16, :]
    columns_out[64:80, :] = coefs[0:16, :]


def operator_kernel(slots, coefs, rows_in, columns_in, weights, offsets, out, faces, spread):
    lane = lanes()
    column = lane % 16
    even = lane % 2 == 0
    bi, bj = device_block(lax.axis_index("chaos"))
    top, bottom = lane < 16, lane >= 112
    left, right = column < 2, column >= 14
    row_edge = ((bi == 0) & top) | ((bi == 3) & bottom)
    column_edge = ((bj == 0) & left) | ((bj == 7) & right)
    row_target = jnp.where(bi == 0, 128, 240)
    column_target = jnp.where(bj == 0, 128, 142)

    def neighbours(block, beside, sides):
        return (
            jnp.where(top, beside, roll(block, 16)),
            jnp.where(bottom, beside, roll(block, -16)),
            jnp.where(left, sides, roll(block, 2)),
            jnp.where(right, sides, roll(block, -2)),
            jnp.where(even, roll(block, -1), roll(block, 1)),
        )

    row_coef = jnp.where(bi == 0, 16, 112)
    column_coef = jnp.where(bj == 0, 114, 14)
    for h in range(2):
        terms = slice(8 * h, 8 * h + 8)
        edge_terms = slice(64 + 8 * h, 72 + 8 * h)
        center = coefs[terms, :]
        beside = jnp.where(
            row_edge, pltpu.roll(rows_in[edge_terms, :], row_coef, 1), coefs[16 + 8 * h : 24 + 8 * h, :]
        )
        sides = jnp.where(
            column_edge, pltpu.roll(columns_in[edge_terms, :], column_coef, 1), coefs[32 + 8 * h : 40 + 8 * h, :]
        )
        for face, other in enumerate(neighbours(center, beside, sides)):
            faces[face, terms, :] = (center + other) * 0.5

    def one_slot(s, carry):
        q, r = s // 4, s % 4
        units = slots[s, 16:24, :]
        opened = spread_units(units, lane)
        halves = []
        for h in range(2):
            block = slots[s, 8 * h : 8 * h + 8, :]
            edge_terms = pl.ds(pl.multiple_of(16 * r + 8 * h, 8), 8)
            beside = roll(units, -(80 + 32 * h))
            beside = jnp.where(
                row_edge, pltpu.roll(rows_in[edge_terms, :], lax.rem(row_target - 16 * q, 128), 1), beside
            )
            sides = jnp.where(column < 8, roll(opened, -(16 + 4 * h)), roll(opened, 12 - 4 * h))
            sides = jnp.where(
                column_edge,
                pltpu.roll(columns_in[edge_terms, :], lax.rem(column_target - 2 * q, 128), 1),
                sides,
            )
            others = neighbours(block, beside, sides)
            halves.append((block, [block - other for other in others]))

        def diffuse(k):
            sums = []
            for block, differences in halves:
                total = faces[0, k : k + 1, :] * differences[0]
                for face in range(1, 5):
                    total = total + faces[face, k : k + 1, :] * differences[face]
                sums.append(total)
            return sums

        for h, total in enumerate(diffuse(0)):
            out[s, 8 * h : 8 * h + 8, :] = halves[h][0] + total
        for k in range(MODES):
            total = jnp.concatenate(diffuse(k + 1), axis=0)
            high = total.astype(bf16)
            low = (total - high.astype(f32)).astype(bf16)
            at = pl.ds(pl.multiple_of(512 * k + 16 * s, 16), 16)
            spread[at, 0:128] = high
            spread[at, 128:256] = low
        return carry

    lax.fori_loop(0, 32, one_slot, 0)

    def one_block(d, carry):
        total = jnp.zeros((64, 256), f32)
        for k in range(MODES):
            shift_one, shift_two = offsets[2 * k], offsets[2 * k + 1]
            gathered = []
            for at in (d + shift_one, d + shift_two, d + 8 - shift_one, d + 8 - shift_two):
                start = pl.multiple_of(512 * k + 64 * lax.rem(at, 8), 64)
                gathered.append(spread[pl.ds(start, 64), :])
            total = total + jnp.dot(
                weights[d, k], jnp.concatenate(gathered, axis=0), preferred_element_type=f32
            )
        mixed = total[:, :128] + total[:, 128:]
        for part in range(4):
            out[4 * d + part] = out[4 * d + part] + mixed[16 * part : 16 * part + 16]
        return carry

    lax.fori_loop(0, 8, one_block, 0, unroll=2)


def finish_kernel(field, slots, lower_bound, upper_bound, out):
    lane = lanes()
    lower_end = jnp.full((8, 128), lower_bound[0], f32)
    upper_end = jnp.full((8, 128), upper_bound[0], f32)
    middle = (upper_end + lower_end) * 0.5
    half_width = (upper_end - lower_end) * 0.5
    spread_ratio = middle / half_width
    factor_now = 1.0 / spread_ratio
    factor_next = 1.0 / (2.0 * spread_ratio - factor_now)
    residual_scale = 2.0 * factor_next / half_width
    field_scale = (1.0 + factor_next * factor_now) / middle + residual_scale
    applied_scale = residual_scale / middle
    for bi in range(4):
        for h in range(2):
            terms = slice(8 * h, 8 * h + 8)
            rows = swap_chunks([slots[block_device(bi, bj), terms, :] for bj in range(8)], lane)
            for i in range(8):
                at = 8 * bi + i
                out[terms, at, :] = field_scale * field[terms, at, :] - applied_scale * rows[i]


def in_vmem():
    return pl.BlockSpec(memory_space=pltpu.VMEM)


def in_smem():
    return pl.BlockSpec(memory_space=pltpu.SMEM)


def call(kernel, ins, outs, scratch=(), cost=None, limit=None):
    return pl.pallas_call(
        kernel,
        out_shape=outs,
        in_specs=ins,
        out_specs=jax.tree.map(lambda _: in_vmem(), outs),
        scratch_shapes=scratch,
        cost_estimate=cost,
        compiler_params=pltpu.CompilerParams(vmem_limit_bytes=limit or 32 * 2**20),
        name=kernel.__name__,
    )


def per_device(right_side, mean_coef, mode_coef, coupling, offsets, lower_bound, upper_bound):
    shape = jax.ShapeDtypeStruct
    slots = call(pack_kernel, [in_vmem()], shape((32, 24, 128), f32))(right_side)
    held = lax.all_to_all(slots, "chaos", 0, 0, tiled=True)
    flat_offsets = offsets.reshape(2 * MODES)
    weights, coefs = call(
        prepare_kernel,
        [in_vmem(), in_smem(), in_vmem(), in_vmem()],
        (shape((8, MODES, 64, 256), bf16), shape((48, 128), f32)),
        [pltpu.VMEM((512, 128), f32), pltpu.VMEM((16, 32, 128), f32), pltpu.VMEM((8, 8, 128), f32)],
        pl.CostEstimate(flops=2**27, bytes_accessed=2**22, transcendentals=0),
    )(coupling.reshape(16 * MODES, 4096), flat_offsets, mean_coef, mode_coef)
    rows_out, columns_out = call(
        edges_kernel, [in_vmem()] * 2, (shape((80, 128), f32), shape((80, 128), f32))
    )(held, coefs)

    def index(device, sx, sy):
        return (device * 4 + sx % 4) * 4 + sy % 4

    row_pairs, column_pairs = [], []
    for sx in range(4):
        for sy in range(4):
            for bj in range(8):
                low, high = block_device(0, bj), block_device(3, bj)
                row_pairs.append((index(high, sx, sy), index(low, sx + 1, sy)))
                row_pairs.append((index(low, sx, sy), index(high, sx - 1, sy)))
            for bi in range(4):
                low, high = block_device(bi, 0), block_device(bi, 7)
                column_pairs.append((index(high, sx, sy), index(low, sx, sy + 1)))
                column_pairs.append((index(low, sx, sy), index(high, sx, sy - 1)))
    axes = ("chaos", "sx", "sy")
    rows_in = lax.ppermute(rows_out, axes, row_pairs)
    columns_in = lax.ppermute(columns_out, axes, column_pairs)
    applied = call(
        operator_kernel,
        [in_vmem()] * 5 + [in_smem()],
        shape((32, 16, 128), f32),
        [pltpu.VMEM((5, 16, 128), f32), pltpu.VMEM((512 * MODES, 256), bf16)],
    )(held, coefs, rows_in, columns_in, weights, flat_offsets)
    returned = lax.all_to_all(applied, "chaos", 0, 0, tiled=True)
    return call(
        finish_kernel,
        [in_vmem()] * 2 + [in_smem()] * 2,
        shape(right_side.shape, f32),
    )(right_side, returned, lower_bound, upper_bound)


def solution(mesh):
    return jax.shard_map(
        per_device,
        mesh=mesh,
        in_specs=(P("chaos", "sx", "sy"), P("sx", "sy"), P(None, "sx", "sy"), P(), P(), P(), P()),
        out_specs=P("chaos", "sx", "sy"),
        check_vma=False,
    )
```

time: 223 us -> 71 us (0.32)
  local copies, waits for them, and re-layouts: 64.6 us -> 4.76 us
  between operations: 53.2 us -> 1.35 us
  other arithmetic: 24.5 us -> 0 us
  starting transfers between devices: 56.1 us -> 32.1 us
  Pallas kernels: 0 us -> 23 us
  matrix products: 13.6 us -> 0 us
    ppermute x8 -> x2, starting transfers between devices: 38.7 us -> 14.3 us  [the longest x1 7.15 us: per_device(): columns_in = lax.ppermute(columns_out, axes, column_pairs)]
    pallas_call x0 -> x5, Pallas kernels: none -> 23 us  [the longest x1 13.5 us: per_device(): call(operator_kernel, [in_vmem()] * 5 + [in_smem()], shape((32, 16, 128),...]
    mul x13 -> x0, local copies, waits for them, and re-layouts: 19.6 us -> none  [the longest x8 14.9 us: per_device(): diffused = diffused + weights[1:, face][:, None] * differences[face][None]]
    another operation x20 -> x0, local copies, waits for them, and re-layouts: 17.2 us -> none  [mix_terms(): coupling[mode_index, diag_index]]
    dot_general x40 -> x0, matrix products: 13.6 us -> none  [the longest x20 7.43 us: mix_terms(): jnp.einsum('dab,dbc->dac', matrix, jnp.roll(source, -shift_by, axis=0), p...]
    slice x15 -> x0, local copies, waits for them, and re-layouts: 13.4 us -> none  [the longest x2 3.53 us: mix_terms(): coupling[mode_index, diag_index]]
    mul x2 -> x0, other arithmetic: 8.92 us -> none  [per_device(): weights = jnp.stack([(center + other) * 0.5 for other in beside], axis=1)]
    add x3 -> x0, other arithmetic: 8.85 us -> none  [the longest x1 5.22 us: per_device(): result = result + weights[0, face][None] * differences[face]]
  transfers between devices with their start and end apart: 10 -> 4, of which waited for: 1 -> 3; matrix products, arithmetic and copies ran while one was open for 32% -> 1% of each run, Pallas kernels for 0% -> 9%
where the time goes in v1:
time: 71 us; the launch traced here: 70.6 us
  starting transfers between devices  32.1 us (45%)
  Pallas kernels  23 us (32%)
  waiting for transfers between devices  9.41 us (13%)
  local copies, waits for them, and re-layouts  4.76 us (7%)
  between operations  1.35 us (2%)
    pallas_call x1, Pallas kernels, per_device(): call(operator_kernel, [in_vmem()] * 5 + [in_smem()], shape((32, 16, 128),...  13.5 us
    all_to_all x1, starting transfers between devices, per_device(): held = lax.all_to_all(slots, 'chaos', 0, 0, tiled=True)  10.4 us
    all_to_all x1, waiting for transfers between devices, per_device(): returned = lax.all_to_all(applied, 'chaos', 0, 0, tiled=True)  7.72 us
    all_to_all x1, starting transfers between devices, per_device(): returned = lax.all_to_all(applied, 'chaos', 0, 0, tiled=True)  7.35 us
    ppermute x1, starting transfers between devices, per_device(): columns_in = lax.ppermute(columns_out, axes, column_pairs)  7.15 us
    ppermute x1, starting transfers between devices, per_device(): rows_in = lax.ppermute(rows_out, axes, row_pairs)  7.14 us
    pallas_call x1, Pallas kernels, per_device(): call(prepare_kernel, [in_vmem(), in_smem(), in_vmem(), in_vmem()], (shape...  6.15 us
    unnamed x11, local copies, waits for them, and re-layouts  4.67 us
  transfers between devices with their start and end apart: 4, of which 3 were waited for; matrix products, arithmetic and copies ran while one was open for 1% of the time, Pallas kernels for 9%

profile of v1, /device:TPU:1, one launch (start us, length us, event | category | flops | bytes accessed | tf_op | source)
XLA Modules:
  0.0 70.6 jit_solution(13841638058649341389)
XLA Ops:
  0.0 0.0 copy-start.1
  0.0 0.9 %copy-done.1 = f32[16,32,128]{2,1,0:T(8,128)S(1)} copy-done((f32[16,32,128]{2,1,0:T(8,128)S(1)}, f32[16,32,128]{2,1,0:T(8,128)}, u32[]{:S(2)}) %copy-start.1) | copy-done | bytes 262168
  1.0 1.9 %pack_kernel.1 = f32[32,24,128]{2,1,0:T(8,128)} custom-call(f32[16,32,128]{2,1,0:T(8,128)S(1)} %copy-done.1), custom_call_target="tpu_custom_call" | custom-call | tf_op jit(solution)/shard_map/pack_kernel/pallas_call | solution.py:304
  2.8 10.4 %all-to-all-start = ((f32[32,24,128]{2,1,0:T(8,128)}), f32[32,24,128]{2,1,0:T(8,128)S(1)}, u32[]{:S(2)}, u32[]{:S(2)}) async-start(f32[32,24,128]{2,1,0:T(8,128)} %pack_kernel.1), calls=%async_computation | async-start | bytes 786432 | tf_op jit(solution)/shard_map/all_to_all | solution.py:305
  13.2 0.8 %copy.9 = s32[10,2]{1,0:T(8,128)S(1)} copy(s32[10,2]{0,1:T(2,128)} %param.11) | data formatting | bytes 160 | tf_op args[4]
  14.0 0.1 reshape.7.offsets
  14.1 0.0 copy-start
  14.1 1.3 %copy-done = bf16[10,2,8,4096]{3,2,1,0:T(8,128)(2,1)S(1)} copy-done((bf16[10,2,8,4096]{3,2,1,0:T(8,128)(2,1)S(1)}, bf16[10,2,8,4096]{3,2,1,0:T(8,128)(2,1)}, u32[]{:S(2)}) %copy-start) | copy-done | bytes 1310744
  15.4 0.0 copy-start.3
  15.4 0.9 %copy-done.3 = f32[10,32,128]{2,1,0:T(8,128)S(1)} copy-done((f32[10,32,128]{2,1,0:T(8,128)S(1)}, f32[10,32,128]{2,1,0:T(8,128)}, u32[]{:S(2)}) %copy-start.3) | copy-done | bytes 163864
  16.3 0.0 copy-start.4
  16.3 0.7 %copy-done.4 = f32[32,128]{1,0:T(8,128)S(1)} copy-done((f32[32,128]{1,0:T(8,128)S(1)}, f32[32,128]{1,0:T(8,128)}, u32[]{:S(2)}) %copy-start.4) | copy-done | bytes 16408
  17.0 0.0 copy-start.2
  17.0 6.1 %prepare_kernel.1 = (bf16[8,10,64,256]{3,2,1,0:T(8,128)(2,1)S(1)}, f32[48,128]{1,0:T(8,128)S(1)}) custom-call(bf16[160,4096]{1,0:T(8,128)(2,1)S(1)} %bitcast.1, s32[20]{0:T(128)S(1)} %reshape.7.offsets, f32[32,128]{1,0:T(8,128)S(1)} %copy-done.4, f32[10,32,128]{2,1,0:T(8,128)S(1)} %copy-done.3), custom_call_target="tpu_custom_call" | custom-call | flops 134217728 | bytes 4194304 | tf_op jit(solution)/shard_map/prepare_kernel/pallas_call | solution.py:307
  23.2 0.3 all-to-all-done.slots
  23.5 0.2 edges_kernel.1
  23.7 7.1 %collective-permute-start = (f32[80,128]{1,0:T(8,128)S(1)}, f32[80,128]{1,0:T(8,128)S(1)}, u32[]{:S(2)}, u32[]{:S(2)}) collective-permute-start(f32[80,128]{1,0:T(8,128)S(1)} %get-tuple-element.10), channel_id=1, source_target_pairs={{16,4},{0,28},{144,132},{128,156},{272,260},{256,284},{400,388},{3... | collective-permute-start | bytes 122888 | tf_op jit(solution)/shard_map/ppermute | solution.py:333
  30.9 7.2 %collective-permute-start.1 = (f32[80,128]{1,0:T(8,128)S(1)}, f32[80,128]{1,0:T(8,128)S(1)}, u32[]{:S(2)}, u32[]{:S(2)}) collective-permute-start(f32[80,128]{1,0:T(8,128)S(1)} %get-tuple-element.11), channel_id=1, source_target_pairs={{32,1},{0,35},{96,65},{64,99},{112,81},{80,115},{48,17},{16,51},{3... | collective-permute-start | bytes 122888 | tf_op jit(solution)/shard_map/ppermute | solution.py:334
  38.0 0.0 collective-permute-done.rows_in
  38.1 1.4 %collective-permute-done.1.columns_in = f32[80,128]{1,0:T(8,128)S(1)} collective-permute-done((f32[80,128]{1,0:T(8,128)S(1)}, f32[80,128]{1,0:T(8,128)S(1)}, u32[]{:S(2)}, u32[]{:S(2)}) %collective-permute-start.1) | collective-permute-done | bytes 40992 | tf_op jit(solution)/shard_map/ppermute | solution.py:334
  39.4 13.5 %operator_kernel.1 = f32[32,16,128]{2,1,0:T(8,128)} custom-call(f32[32,24,128]{2,1,0:T(8,128)S(1)} %all-to-all-done.slots, f32[48,128]{1,0:T(8,128)S(1)} %get-tuple-element.9.coefs, f32[80,128]{1,0:T(8,128)S(1)} %collective-permute-done.rows_in, f32[80,128]{1,0:T(8,128)S(1)} %collective-permute-done.1.columns_in, ...), custom_call_target="tpu_custom_call" | custom-call | tf_op jit(solution)/shard_map/operator_kernel/pallas_call | solution.py:335
  52.9 7.4 %all-to-all-start.1 = ((f32[32,16,128]{2,1,0:T(8,128)}), f32[32,16,128]{2,1,0:T(8,128)S(1)}, u32[]{:S(2)}, u32[]{:S(2)}) async-start(f32[32,16,128]{2,1,0:T(8,128)} %operator_kernel.1), calls=%async_computation.1 | async-start | bytes 524288 | tf_op jit(solution)/shard_map/all_to_all | solution.py:341
  61.6 7.7 %all-to-all-done.1.slots = f32[32,16,128]{2,1,0:T(8,128)S(1)} async-done(((f32[32,16,128]{2,1,0:T(8,128)}), f32[32,16,128]{2,1,0:T(8,128)S(1)}, u32[]{:S(2)}, u32[]{:S(2)}) %all-to-all-start.1) | async-done | bytes 262176 | tf_op jit(solution)/shard_map/all_to_all | solution.py:341
  69.3 0.0 copy-done.2
  69.3 1.2 %finish_kernel.1 = f32[16,32,128]{2,1,0:T(8,128)} custom-call(f32[16,32,128]{2,1,0:T(8,128)S(1)} %copy-done.2, f32[32,16,128]{2,1,0:T(8,128)S(1)} %all-to-all-done.1.slots, f32[1]{0:T(128)S(6)} %copy.10.lower_bound, f32[1]{0:T(128)S(6)} %copy.11.upper_bound), custom_call_target="tpu_custom_call" | custom-call | tf_op jit(solution)/shard_map/finish_kernel/pallas_call | solution.py:342
Async XLA Ops:
  0.0 0.9 %copy-start.1 = (f32[16,32,128]{2,1,0:T(8,128)S(1)}, f32[16,32,128]{2,1,0:T(8,128)}, u32[]{:S(2)}) copy-start(f32[16,32,128]{2,1,0:T(8,128)} %field.3) | copy-start | bytes 786436
  2.8 20.7 %all-to-all-start = ((f32[32,24,128]{2,1,0:T(8,128)}), f32[32,24,128]{2,1,0:T(8,128)S(1)}, u32[]{:S(2)}, u32[]{:S(2)}) async-start(f32[32,24,128]{2,1,0:T(8,128)} %pack_kernel.1), calls=%async_computation | async-start | bytes 786432 | tf_op jit(solution)/shard_map/all_to_all | solution.py:305
  14.1 1.3 %copy-start = (bf16[10,2,8,4096]{3,2,1,0:T(8,128)(2,1)S(1)}, bf16[10,2,8,4096]{3,2,1,0:T(8,128)(2,1)}, u32[]{:S(2)}) copy-start(bf16[10,2,8,4096]{3,2,1,0:T(8,128)(2,1)} %param.10) | copy-start | bytes 3932164
  15.4 0.9 %copy-start.3 = (f32[10,32,128]{2,1,0:T(8,128)S(1)}, f32[10,32,128]{2,1,0:T(8,128)}, u32[]{:S(2)}) copy-start(f32[10,32,128]{2,1,0:T(8,128)} %mode_coef.1) | copy-start | bytes 491524
  16.3 0.7 %copy-start.4 = (f32[32,128]{1,0:T(8,128)S(1)}, f32[32,128]{1,0:T(8,128)}, u32[]{:S(2)}) copy-start(f32[32,128]{1,0:T(8,128)} %mean_coef.1) | copy-start | bytes 49156
  17.0 52.3 %copy-start.2 = (f32[16,32,128]{2,1,0:T(8,128)S(1)}, f32[16,32,128]{2,1,0:T(8,128)}, u32[]{:S(2)}) copy-start(f32[16,32,128]{2,1,0:T(8,128)} %field.3) | copy-start | bytes 786436
  23.7 14.3 %collective-permute-start = (f32[80,128]{1,0:T(8,128)S(1)}, f32[80,128]{1,0:T(8,128)S(1)}, u32[]{:S(2)}, u32[]{:S(2)}) collective-permute-start(f32[80,128]{1,0:T(8,128)S(1)} %get-tuple-element.10), channel_id=1, source_target_pairs={{16,4},{0,28},{144,132},{128,156},{272,260},{256,284},{400,388},{3... | collective-permute-start | bytes 122888 | tf_op jit(solution)/shard_map/ppermute | solution.py:333
  30.9 8.5 %collective-permute-start.1 = (f32[80,128]{1,0:T(8,128)S(1)}, f32[80,128]{1,0:T(8,128)S(1)}, u32[]{:S(2)}, u32[]{:S(2)}) collective-permute-start(f32[80,128]{1,0:T(8,128)S(1)} %get-tuple-element.11), channel_id=1, source_target_pairs={{32,1},{0,35},{96,65},{64,99},{112,81},{80,115},{48,17},{16,51},{3... | collective-permute-start | bytes 122888 | tf_op jit(solution)/shard_map/ppermute | solution.py:334
  52.9 16.4 %all-to-all-start.1 = ((f32[32,16,128]{2,1,0:T(8,128)}), f32[32,16,128]{2,1,0:T(8,128)S(1)}, u32[]{:S(2)}, u32[]{:S(2)}) async-start(f32[32,16,128]{2,1,0:T(8,128)} %operator_kernel.1), calls=%async_computation.1 | async-start | bytes 524288 | tf_op jit(solution)/shard_map/all_to_all | solution.py:341

commit v2 on v1

v2 whole, which is shorter than its diff:
```python
import functools

import jax
import jax.numpy as jnp
from jax import lax
from jax.experimental import pallas as pl
from jax.experimental.pallas import tpu as pltpu
from jax.sharding import PartitionSpec as P

f32 = jnp.float32
bf16 = jnp.bfloat16
MODES = 10


def block_device(bi, bj):
    core = (0, 0, 1, 1)[bi]
    outer = bi in (0, 3)
    if bj < 4:
        x, y = (0 if outer else 1), bj
    else:
        x, y = (3 if outer else 2), 7 - bj
    return y * 8 + x * 2 + core


def device_block(index):
    core, x, y = index % 2, (index // 2) % 4, index // 8
    bi = jnp.where((x == 0) | (x == 3), 3 * core, 1 + core)
    bj = jnp.where(x < 2, y, 7 - y)
    return bi, bj


def lane_numbers():
    return lax.broadcasted_iota(jnp.int32, (8, 128), 1)


def roll(value, shift):
    if isinstance(shift, int):
        shift = shift % 128
        if shift == 0:
            return value
    return pltpu.roll(value, shift, 1)


def chunk_masks(lane):
    return {step: lane & (16 * step) == 0 for step in (1, 2, 4)}


def swap_chunks(rows, low):
    rows = list(rows)
    for step in (1, 2, 4):
        for i in range(8):
            if i & step == 0:
                a, b = rows[i], rows[i + step]
                rows[i] = jnp.where(low[step], a, roll(b, 16 * step))
                rows[i + step] = jnp.where(low[step], roll(a, -16 * step), b)
    return rows


def unit_masks(lane):
    return lane & 31 < 8, lane & 63 < 16, lane < 32


def pack_kernel(source, target, field, slots, arrived, left):
    copies = [
        pltpu.make_async_copy(
            source.at[:, 8 * bi : 8 * bi + 8, :], field.at[:, 8 * bi : 8 * bi + 8, :], arrived.at[bi]
        )
        for bi in range(4)
    ]
    for copy in copies:
        copy.start()
    lane = lane_numbers()
    low = chunk_masks(lane)
    unit_first, unit_second, unit_third = unit_masks(lane)
    column = lane & 15
    upper, unit_half = column >= 8, column < 4
    next_place = [(lane >> 4) == 4 + 2 * h for h in range(2)]
    last_place = [(lane >> 4) == 5 + 2 * h for h in range(2)]
    for copy in copies:
        copy.wait()
    leaving = []
    for bi in range(4):
        blocks, above, below = [], [], []
        for h in range(2):
            terms = slice(8 * h, 8 * h + 8)
            rows = [field[terms, 8 * bi + i, :] for i in range(8)]
            blocks.append(swap_chunks(rows, low))
            above.append(field[terms, 8 * bi - 1, :] if bi > 0 else rows[0])
            below.append(field[terms, 8 * bi + 8, :] if bi < 3 else rows[7])
        for bj in range(8):
            at = block_device(bi, bj)
            units = []
            for h in range(2):
                slots[at, 8 * h : 8 * h + 8, :] = blocks[h][bj]
                side = jnp.where(upper, blocks[h][(bj - 1) % 8], blocks[h][(bj + 1) % 8])
                units.append(roll(side, 2 + 4 * h))
            row = jnp.where(unit_half, units[0], units[1])
            row = jnp.where(unit_first, row, roll(row, -8))
            row = jnp.where(unit_second, row, roll(row, -16))
            row = jnp.where(unit_third, row, roll(row, -32))
            for h in range(2):
                start = 64 + 32 * h
                row = jnp.where(next_place[h], roll(below[h], start - 16 * bj), row)
                row = jnp.where(last_place[h], roll(above[h], start + 16 - 16 * bj), row)
            slots[at, 16:24, :] = row
        for bj in range(8):
            at = block_device(bi, bj)
            leaving.append(pltpu.make_async_copy(slots.at[at], target.at[at], left.at[at]))
            leaving[-1].start()
    for copy in leaving:
        copy.wait()


def prepare_kernel(
    coupling_at, offsets, mean_at, mode_at, weights, coefs, coupling, pairs, tile, parts, arrived
):
    copies = [
        pltpu.make_async_copy(mean_at, tile.at[0], arrived.at[0]),
        pltpu.make_async_copy(mode_at, tile.at[1 : MODES + 1], arrived.at[1]),
        pltpu.make_async_copy(coupling_at, coupling, arrived.at[2]),
    ]
    for copy in copies:
        copy.start()
    tile[MODES + 1 :] = jnp.zeros((15 - MODES, 32, 128), f32)
    lane = lane_numbers()
    low = chunk_masks(lane)
    first = lane < 64
    left_half = lane & 15 < 8
    bi, bj = device_block(lax.axis_index("chaos"))
    copies[0].wait()
    copies[1].wait()
    for h in range(2):
        terms = slice(8 * h, 8 * h + 8)
        blocks = swap_chunks([tile[terms, 8 * bi + i, :] for i in range(8)], low)
        for j in range(8):
            parts[j] = blocks[j]
        coefs[8 * h : 8 * h + 8, :] = parts[bj]
        above = tile[terms, lax.rem(8 * bi + 31, 32), :]
        below = tile[terms, lax.rem(8 * bi + 8, 32), :]
        coefs[16 + 8 * h : 24 + 8 * h, :] = jnp.where(
            first,
            pltpu.roll(above, lax.rem(128 - 16 * bj, 128), 1),
            pltpu.roll(below, lax.rem(240 - 16 * bj, 128), 1),
        )
        coefs[32 + 8 * h : 40 + 8 * h, :] = jnp.where(
            left_half, roll(parts[lax.rem(bj + 7, 8)], -14), roll(parts[lax.rem(bj + 1, 8)], 14)
        )
    out_row = lax.broadcasted_iota(jnp.int32, (64, 128), 0)
    out_col = lax.broadcasted_iota(jnp.int32, (64, 128), 1)
    pick = jnp.where(out_col & 63 == out_row, 1.0, 0.0).astype(bf16)
    wide = out_col < 64
    copies[2].wait()

    def one_mode(k, carry):
        base = pl.multiple_of(512 * k, 512)
        for m in range(32):
            both = coupling[pl.ds(pl.multiple_of(16 * k, 16), 16), 128 * m : 128 * m + 128].astype(f32)
            one, two = both[:8], both[8:]
            pairs[pl.ds(base + 2 * m, 8, 64), :] = jnp.where(first, one, roll(two, 64))
            pairs[pl.ds(base + 2 * m + 1, 8, 64), :] = jnp.where(first, roll(one, 64), two)
        shift_one, shift_two = offsets[0, k], offsets[1, k]
        for d in range(8):
            weights[d, k, :, 0:128] = pairs[pl.ds(base + 64 * d, 64), :].astype(bf16)
            from_one = lax.rem(d + 8 - shift_one, 8)
            from_two = lax.rem(d + 8 - shift_two, 8)
            one = pairs[pl.ds(pl.multiple_of(base + 64 * from_one, 64), 64), :]
            two = pairs[pl.ds(pl.multiple_of(base + 64 * from_two, 64), 64), :]
            stack = jnp.concatenate([jnp.where(wide, one, 0.0), jnp.where(wide, 0.0, two)], axis=0)
            turned = lax.dot_general(
                pick, stack.astype(bf16), (((1,), (1,)), ((), ())), preferred_element_type=f32
            )
            weights[d, k, :, 128:256] = turned.astype(bf16)
        return carry

    lax.fori_loop(0, MODES, one_mode, 0, unroll=2)


def send_kernel(along_rows, slots, coefs, *rest):
    lane = lane_numbers()
    bi, bj = device_block(lax.axis_index("chaos"))
    if along_rows:
        shift, stride, place = jnp.where(bi == 0, 0, 16), 16, lane >> 4
    else:
        shift, stride, place = jnp.where(bj == 0, 0, 114), 2, (lane & 15) >> 1
    sent = rest[-1]
    for r in range(8):
        total = jnp.zeros((8, 128), f32)
        for q in range(8):
            at, h = 4 * q + r // 2, r % 2
            block = slots[at, 8 * h : 8 * h + 8, :]
            total = jnp.where(place == q, pltpu.roll(block, lax.rem(shift + stride * q, 128), 1), total)
        sent[8 * r : 8 * r + 8, :] = total
    sent[64:80, :] = coefs[0:16, :]


def gather_blocks(spread, offsets, k, d):
    rows = []
    shift_one, shift_two = offsets[0, k], offsets[1, k]
    for at in (d + shift_one, d + shift_two, d + 8 - shift_one, d + 8 - shift_two):
        start = pl.multiple_of(512 * k + 64 * lax.rem(at, 8), 64)
        rows.append(spread[pl.ds(start, 64), :])
    return jnp.concatenate(rows, axis=0)


def again_kernel(columns_out, after, sent):
    sent[...] = columns_out[...]


def inner_kernel(slots, coefs, weights, offsets_at, after, also_after, out, faces, spread, offsets, arrived):
    copy = pltpu.make_async_copy(offsets_at, offsets, arrived.at[0])
    copy.start()
    inner_operator(slots, coefs, weights, offsets, copy, out, faces, spread)


def inner_operator(slots, coefs, weights, offsets, offsets_copy, out, faces, spread):
    lane = lane_numbers()
    column = lane & 15
    even = lane & 1 == 0
    bi, bj = device_block(lax.axis_index("chaos"))
    top, bottom = lane < 16, lane >= 112
    left, right = column < 2, column >= 14
    left_half = column < 8
    unit_first, unit_second, unit_third = unit_masks(lane)
    row_edge = ((bi == 0) & top) | ((bi == 3) & bottom)
    column_edge = ((bj == 0) & left) | ((bj == 7) & right)

    def neighbours(block, beside, sides):
        return (
            jnp.where(top, beside, roll(block, 16)),
            jnp.where(bottom, beside, roll(block, -16)),
            jnp.where(left, sides, roll(block, 2)),
            jnp.where(right, sides, roll(block, -2)),
            jnp.where(even, roll(block, -1), roll(block, 1)),
        )

    for h in range(2):
        center = coefs[8 * h : 8 * h + 8, :]
        beside = coefs[16 + 8 * h : 24 + 8 * h, :]
        sides = coefs[32 + 8 * h : 40 + 8 * h, :]
        for face, other in enumerate(neighbours(center, beside, sides)):
            weight = (center + other) * 0.5
            for k in range(8 * h, min(8 * h + 8, MODES + 1)):
                faces[5 * k + face] = jnp.broadcast_to(weight[k - 8 * h : k - 8 * h + 1], (8, 128))

    def one_slot(s, carry):
        units = slots[s, 16:24, :]
        opened = jnp.where(unit_third, units, roll(units, 32))
        opened = jnp.where(unit_second, opened, roll(opened, 16))
        opened = jnp.where(unit_first, opened, roll(opened, 8))
        halves = []
        for h in range(2):
            block = slots[s, 8 * h : 8 * h + 8, :]
            beside = jnp.where(row_edge, block, roll(units, -(80 + 32 * h)))
            sides = jnp.where(left_half, roll(opened, -(16 + 4 * h)), roll(opened, 12 - 4 * h))
            sides = jnp.where(column_edge, block, sides)
            others = neighbours(block, beside, sides)
            halves.append((block, [block - other for other in others]))

        def diffuse(k):
            sums = []
            for block, steps in halves:
                total = faces[5 * k] * steps[0]
                for face in range(1, 5):
                    total = total + faces[5 * k + face] * steps[face]
                sums.append(total)
            return sums

        for h, total in enumerate(diffuse(0)):
            out[s, 8 * h : 8 * h + 8, :] = halves[h][0] + total
        for k in range(MODES):
            total = jnp.concatenate(diffuse(k + 1), axis=0)
            high = total.astype(bf16)
            low = (total - high.astype(f32)).astype(bf16)
            at = pl.ds(pl.multiple_of(512 * k + 16 * s, 16), 16)
            spread[at, 0:128] = high
            spread[at, 128:256] = low
        return carry

    lax.fori_loop(0, 32, one_slot, 0, unroll=8)
    offsets_copy.wait()

    def one_block(d, carry):
        total = jnp.zeros((64, 256), f32)
        for k in range(MODES):
            blocks = gather_blocks(spread, offsets, k, d)
            total = total + jnp.dot(weights[d, k], blocks, preferred_element_type=f32)
        mixed = total[:, :128] + total[:, 128:]
        for part in range(4):
            out[4 * d + part] = out[4 * d + part] + mixed[16 * part : 16 * part + 16]
        return carry

    lax.fori_loop(0, 8, one_block, 0, unroll=8)


def wait_blocks(source, target, left):
    for d in range(8):
        part = slice(4 * d, 4 * d + 4)
        pltpu.make_async_copy(source.at[part], target.at[part], left.at[d]).wait()


def edge_kernel(rows_out, rows_in, columns_out, columns_first, columns_later, weights, offsets_at, inner, target, steps, spread, columns_in, out, left,
    offsets, arrived,
):
    bi, bj = device_block(lax.axis_index("chaos"))
    on_row = (bi == 0) | (bi == 3)
    on_column = (bj == 0) | (bj == 7)
    offsets_copy = pltpu.make_async_copy(offsets_at, offsets, arrived.at[0])
    offsets_copy.start()

    @pl.when(jnp.logical_not(on_row | on_column))
    def _():
        copy = pltpu.make_async_copy(inner, target, left.at[0])
        copy.start()
        copy.wait()
        offsets_copy.wait()

    early = lax.axis_index("sx") == 0

    @pl.when(on_column & early)
    def _():
        columns_in[...] = columns_first[...]

    @pl.when(jnp.logical_not(on_column & early))
    def _():
        columns_in[...] = columns_later[...]

    @pl.when(on_row | on_column)
    def _():
        edge_faces(
            bi, bj, on_row, on_column, rows_out, rows_in, columns_out, columns_in, weights, offsets, inner, out, steps, spread, target, left,
            offsets_copy,
        )
        wait_blocks(out, target, left)


def edge_faces(
    bi, bj, on_row, on_column, rows_out, rows_in, columns_out, columns_in, weights, offsets, inner, out, steps, spread,
    target, left, offsets_copy,
):
    lane = lane_numbers()
    column = lane & 15
    for r in range(8):
        rows = slice(8 * r, 8 * r + 8)
        step = rows_out[rows, :] - rows_in[rows, :]
        for bit in (1, 2, 4):
            outer, inner_bit = lane & (16 * bit) != 0, lane & (2 * bit) != 0
            step = jnp.where(
                outer == inner_bit, step, jnp.where(outer, roll(step, 14 * bit), roll(step, -14 * bit))
            )
        steps[rows, :] = step
        steps[64 + 8 * r : 72 + 8 * r, :] = columns_out[rows, :] - columns_in[rows, :]
    row_own, row_other = jnp.where(bi == 0, 0, 16), jnp.where(bi == 0, 16, 0)
    column_own, column_other = jnp.where(bj == 0, 0, 114), jnp.where(bj == 0, 114, 0)
    row_share = jnp.where(on_row, 0.5, 0.0)
    column_share = jnp.where(on_column, 0.5, 0.0)
    factors = []
    for h in range(2):
        terms = slice(64 + 8 * h, 72 + 8 * h)
        row = pltpu.roll(rows_out[terms, :], row_own, 1) + pltpu.roll(rows_in[terms, :], row_other, 1)
        row = jnp.where(lane < 8, row, roll(row, 56))
        row = jnp.where(lane & 63 < 4, row, roll(row, 28))
        row = jnp.where(lane & 31 < 2, row, roll(row, 14))
        side = pltpu.roll(columns_out[terms, :], column_own, 1) + pltpu.roll(
            columns_in[terms, :], column_other, 1
        )
        row, side = row * row_share, side * column_share
        joined = jnp.where(column < 2, side, roll(side, 2))
        joined = jnp.where(column < 4, joined, jnp.where(column < 6, roll(row, 4), roll(row, 6)))
        factors.append(jnp.where(column < 8, joined, 0.0))
    wide_factors = [
        jnp.broadcast_to(factors[k // 8][k % 8 : k % 8 + 1, :], (8, 128)) for k in range(MODES + 1)
    ]
    low_part = column & 2 != 0
    first_two, first_four, first_six = column < 2, column < 4, column < 6

    def scaled(k, step):
        return wide_factors[k] * step

    for q in range(8):
        for r in range(4):
            halves = []
            for half in range(2):
                at = 8 * (2 * r + half)
                row, side = steps[at : at + 8, :], steps[64 + at : 72 + at, :]
                step = jnp.where(first_two, roll(side, -2 * q), roll(side, 2 - 2 * q))
                other = jnp.where(first_six, roll(row, 4 - 2 * q), roll(row, 6 - 2 * q))
                halves.append(jnp.where(first_four, step, other))
            at = 64 * q + 16 * r
            for k in range(MODES):
                parts = []
                for step in halves:
                    total = scaled(k + 1, step)
                    high = total.astype(bf16).astype(f32)
                    parts.append(jnp.where(low_part, total - high, total))
                spread[512 * k + at : 512 * k + at + 16, :] = jnp.concatenate(parts, axis=0).astype(bf16)
            for half, step in enumerate(halves):
                start = 128 + at + 8 * half
                steps[start : start + 8, :] = jnp.where(low_part, 0.0, scaled(0, step))
    from_lane = lax.broadcasted_iota(jnp.int32, (128, 128), 0)
    to_lane = lax.broadcasted_iota(jnp.int32, (128, 128), 1)
    from_column, from_row, plane = from_lane & 15, from_lane >> 4, from_lane & 1
    side_to = 16 * from_row + jnp.where(bj == 0, 0, 14) + plane
    row_to = jnp.where(bi == 0, 0, 112) + 2 * from_row + plane
    lands = jnp.where(from_column < 4, side_to, row_to)
    place = jnp.where((from_column < 8) & (lands == to_lane), 1.0, 0.0).astype(bf16)
    place = jnp.concatenate([place] * 3, axis=0)
    offsets_copy.wait()

    def one_block(d, carry):
        total = steps[pl.ds(pl.multiple_of(128 + 64 * d, 64), 64), :]
        for k in range(MODES):
            blocks = gather_blocks(spread, offsets, k, d)
            total = total + jnp.dot(weights[d, k], blocks, preferred_element_type=f32)
        high = total.astype(bf16)
        rest = total - high.astype(f32)
        middle = rest.astype(bf16)
        low = (rest - middle.astype(f32)).astype(bf16)
        placed = jnp.dot(jnp.concatenate([high, middle, low], axis=1), place, preferred_element_type=f32)
        for part in range(4):
            out[4 * d + part] = inner[4 * d + part] + placed[16 * part : 16 * part + 16]
        pltpu.make_async_copy(out.at[pl.ds(4 * d, 4)], target.at[pl.ds(4 * d, 4)], left.at[d]).start()
        return carry

    lax.fori_loop(0, 8, one_block, 0, unroll=8)


def finish_kernel(field, slots, lower_bound, upper_bound, target, out, left):
    low = chunk_masks(lane_numbers())
    lower_end = jnp.full((8, 128), lower_bound[0], f32)
    upper_end = jnp.full((8, 128), upper_bound[0], f32)
    middle = (upper_end + lower_end) * 0.5
    half_width = (upper_end - lower_end) * 0.5
    spread_ratio = middle / half_width
    factor_now = 1.0 / spread_ratio
    factor_next = 1.0 / (2.0 * spread_ratio - factor_now)
    residual_scale = 2.0 * factor_next / half_width
    field_scale = (1.0 + factor_next * factor_now) / middle + residual_scale
    applied_scale = residual_scale / middle
    copies = []
    for bi in range(4):
        for h in range(2):
            terms = slice(8 * h, 8 * h + 8)
            rows = swap_chunks([slots[block_device(bi, bj), terms, :] for bj in range(8)], low)
            for i in range(8):
                at = 8 * bi + i
                out[terms, at, :] = field_scale * field[terms, at, :] - applied_scale * rows[i]
        part = pl.ds(8 * bi, 8)
        copies.append(pltpu.make_async_copy(out.at[:, part, :], target.at[:, part, :], left.at[bi]))
        copies[-1].start()
    for copy in copies:
        copy.wait()


def from_hbm(array):
    return pltpu.with_memory_space_constraint(array, pltpu.HBM)


def in_any():
    return pl.BlockSpec(memory_space=pl.ANY)


def in_hbm():
    return pl.BlockSpec(memory_space=pltpu.HBM)


def in_vmem():
    return pl.BlockSpec(memory_space=pltpu.VMEM)


def in_smem():
    return pl.BlockSpec(memory_space=pltpu.SMEM)


def call(kernel, ins, outs, scratch=(), cost=None, limit=32, aliases=None, name=None, out_specs=None):
    return pl.pallas_call(
        kernel,
        out_shape=outs,
        in_specs=ins,
        out_specs=out_specs or jax.tree.map(lambda _: in_vmem(), outs),
        scratch_shapes=scratch,
        cost_estimate=cost,
        input_output_aliases=aliases or {},
        compiler_params=pltpu.CompilerParams(vmem_limit_bytes=limit * 2**20),
        name=name or kernel.__name__,
    )


def per_device(right_side, mean_coef, mode_coef, coupling, offsets, lower_bound, upper_bound):
    shape = jax.ShapeDtypeStruct
    slots = call(
        pack_kernel,
        [in_hbm()],
        pltpu.HBM((32, 24, 128), f32),
        [
            pltpu.VMEM((16, 32, 128), f32),
            pltpu.VMEM((32, 24, 128), f32),
            pltpu.SemaphoreType.DMA((4,)),
            pltpu.SemaphoreType.DMA((32,)),
        ],
        out_specs=in_hbm(),
        limit=32,
    )(from_hbm(right_side))
    held = lax.all_to_all(slots, "chaos", 0, 0, tiled=True)
    offsets = offsets.T
    weights, coefs = call(
        prepare_kernel,
        [in_hbm(), in_smem(), in_hbm(), in_hbm()],
        (pltpu.VMEM((8, MODES, 64, 256), bf16), pltpu.VMEM((48, 128), f32)),
        [
            pltpu.VMEM((16 * MODES, 4096), bf16),
            pltpu.VMEM((512 * MODES, 128), f32),
            pltpu.VMEM((16, 32, 128), f32),
            pltpu.VMEM((8, 8, 128), f32),
            pltpu.SemaphoreType.DMA((3,)),
        ],
        pl.CostEstimate(flops=2**27, bytes_accessed=2**22, transcendentals=0),
        limit=32,
    )(from_hbm(coupling.reshape(16 * MODES, 4096)), offsets, from_hbm(mean_coef), from_hbm(mode_coef))
    def index(device, sx, sy):
        return (device * 4 + sx % 4) * 4 + sy % 4

    row_pairs, early_pairs, late_pairs = [], [], []
    for sx in range(4):
        for sy in range(4):
            for bj in range(8):
                low, high = block_device(0, bj), block_device(3, bj)
                row_pairs.append((index(high, sx, sy), index(low, sx + 1, sy)))
                row_pairs.append((index(low, sx, sy), index(high, sx - 1, sy)))
            for bi in range(4):
                low, high = block_device(bi, 0), block_device(bi, 7)
                pairs = early_pairs if sx == 0 else late_pairs
                pairs.append((index(high, sx, sy), index(low, sx, sy + 1)))
                pairs.append((index(low, sx, sy), index(high, sx, sy - 1)))
    axes = ("chaos", "sx", "sy")
    message = shape((80, 128), f32)
    offsets_scratch = [pltpu.SMEM((2, MODES), jnp.int32), pltpu.SemaphoreType.DMA((1,))]
    scratch = [
        pltpu.VMEM((5 * MODES + 5, 8, 128), f32),
        pltpu.VMEM((512 * MODES, 256), bf16),
    ] + offsets_scratch
    inner_cost = pl.CostEstimate(flops=2**32, bytes_accessed=2**24, transcendentals=0)
    inner_shape = pltpu.VMEM((32, 16, 128), f32)
    columns_out = call(
        functools.partial(send_kernel, False), [in_vmem()] * 2 + [in_any()], message, name="send_columns"
    )(held, coefs, coefs)
    columns_first = lax.ppermute(columns_out, axes, early_pairs)
    rows_out = call(
        functools.partial(send_kernel, True), [in_vmem()] * 2 + [in_any()], message, name="send_rows"
    )(held, coefs, columns_out)
    rows_in = lax.ppermute(rows_out, axes, row_pairs)
    columns_again = call(again_kernel, [in_vmem(), in_any()], message, name="send_again")(
        columns_out, rows_out
    )
    columns_later = lax.ppermute(columns_again, axes, late_pairs)
    inner = call(
        inner_kernel,
        [in_vmem()] * 3 + [in_any()] * 3,
        inner_shape,
        scratch,
        inner_cost,
    )(held, coefs, weights, offsets, columns_again, columns_first)
    applied = call(
        edge_kernel,
        [in_vmem()] * 6 + [in_any(), in_vmem()],
        pltpu.HBM((32, 16, 128), f32),
        [
            pltpu.VMEM((128 + 512, 128), f32),
            pltpu.VMEM((512 * MODES, 128), bf16),
            pltpu.VMEM((80, 128), f32),
            pltpu.VMEM((32, 16, 128), f32),
            pltpu.SemaphoreType.DMA((8,)),
        ]
        + offsets_scratch,
        out_specs=in_hbm(),
    )(rows_out, rows_in, columns_out, columns_first, columns_later, weights, offsets, inner)
    returned = lax.all_to_all(applied, "chaos", 0, 0, tiled=True)
    return call(
        finish_kernel,
        [in_vmem()] * 2 + [in_smem()] * 2,
        pltpu.HBM(right_side.shape, f32),
        [pltpu.VMEM(right_side.shape, f32), pltpu.SemaphoreType.DMA((4,))],
        out_specs=in_hbm(),
    )(right_side, returned, lower_bound, upper_bound)


def solution(mesh):
    return jax.shard_map(
        per_device,
        mesh=mesh,
        in_specs=(P("chaos", "sx", "sy"), P("sx", "sy"), P(None, "sx", "sy"), P(), P(), P(), P()),
        out_specs=P("chaos", "sx", "sy"),
        check_vma=False,
    )
```

time: 71 us -> 58.6 us (0.83)
  starting transfers between devices: 32.1 us -> 24.4 us
  Pallas kernels: 23 us -> 18.5 us
  local copies, waits for them, and re-layouts: 4.76 us -> 0.68 us
  waiting for transfers between devices: 9.41 us -> 13.1 us
    ppermute x1, starting transfers between devices: 7.14 us -> 2.49 us  [per_device(): rows_in = lax.ppermute(rows_out, axes, row_pairs)]
    pallas_call x5 -> x8, Pallas kernels: 23 us -> 18.5 us  [the longest x1 6.05 us: per_device(): call(prepare_kernel, [in_hbm(), in_smem(), in_hbm(), in_hbm()], (pltpu.VM...]
    unnamed x11 -> x6, local copies, waits for them, and re-layouts: 4.67 us -> 0.68 us
    all_to_all x1, waiting for transfers between devices: 0.33 us -> 3.54 us  [per_device(): held = lax.all_to_all(slots, 'chaos', 0, 0, tiled=True)]
    ppermute x1, waiting for transfers between devices: 0.01 us -> 1.93 us  [per_device(): rows_in = lax.ppermute(rows_out, axes, row_pairs)]
    all_to_all x1, starting transfers between devices: 7.35 us -> 5.51 us  [per_device(): returned = lax.all_to_all(applied, 'chaos', 0, 0, tiled=True)]
    ppermute x1 -> x2, waiting for transfers between devices: 1.37 us -> 0.01 us  [the longest x1 0.01 us: per_device(): columns_later = lax.ppermute(columns_again, axes, late_pairs)]
    ppermute x1 -> x2, starting transfers between devices: 7.15 us -> 5.98 us  [the longest x1 5.31 us: per_device(): columns_first = lax.ppermute(columns_out, axes, early_pairs)]
  transfers between devices with their start and end apart: 4 -> 5, of which waited for: 3 -> 3; matrix products, arithmetic and copies ran while one was open for 1% -> 0% of each run, Pallas kernels for 9% -> 18%
where the time goes in v2:
time: 58.6 us; the launch traced here: 58.1 us
  starting transfers between devices  24.4 us (42%)
  Pallas kernels  18.5 us (32%)
  waiting for transfers between devices  13.1 us (22%)
  between operations  1.42 us (2%)
  local copies, waits for them, and re-layouts  0.68 us (1%)
    all_to_all x1, starting transfers between devices, per_device(): held = lax.all_to_all(slots, 'chaos', 0, 0, tiled=True)  10.4 us
    all_to_all x1, waiting for transfers between devices, per_device(): returned = lax.all_to_all(applied, 'chaos', 0, 0, tiled=True)  7.66 us
    pallas_call x1, Pallas kernels, per_device(): call(prepare_kernel, [in_hbm(), in_smem(), in_hbm(), in_hbm()], (pltpu.VM...  6.05 us
    all_to_all x1, starting transfers between devices, per_device(): returned = lax.all_to_all(applied, 'chaos', 0, 0, tiled=True)  5.51 us
    ppermute x1, starting transfers between devices, per_device(): columns_first = lax.ppermute(columns_out, axes, early_pairs)  5.31 us
    pallas_call x1, Pallas kernels, per_device(): call(inner_kernel, [in_vmem()] * 3 + [in_any()] * 3, inner_shape, scratch...  4.2 us
    pallas_call x1, Pallas kernels, per_device(): call(edge_kernel, [in_vmem()] * 6 + [in_any(), in_vmem()], pltpu.HBM((32,...  3.79 us
    all_to_all x1, waiting for transfers between devices, per_device(): held = lax.all_to_all(slots, 'chaos', 0, 0, tiled=True)  3.54 us
  transfers between devices with their start and end apart: 5, of which 3 were waited for; matrix products, arithmetic and copies ran while one was open for 0% of the time, Pallas kernels for 18%

profile of v2, /device:TPU:1, one launch (start us, length us, event | category | flops | bytes accessed | tf_op | source)
XLA Modules:
  0.0 58.1 jit_solution(10139481992251031928)
XLA Ops:
  0.0 0.0 copy-start.2
  0.0 2.9 %pack_kernel.1 = f32[32,24,128]{2,1,0:T(8,128)} custom-call(f32[16,32,128]{2,1,0:T(8,128)} %field.1), custom_call_target="tpu_custom_call" | custom-call | tf_op jit(solution)/shard_map/pack_kernel/pallas_call | solution.py:490
  2.9 10.4 %all-to-all-start = ((f32[32,24,128]{2,1,0:T(8,128)}), f32[32,24,128]{2,1,0:T(8,128)S(1)}, u32[]{:S(2)}, u32[]{:S(2)}) async-start(f32[32,24,128]{2,1,0:T(8,128)} %pack_kernel.1), calls=%async_computation | async-start | bytes 786432 | tf_op jit(solution)/shard_map/all_to_all | solution.py:503
  13.3 0.0 copy-start.1
  13.4 0.7 %copy-done.1 = s32[10,2]{0,1:T(2,128)S(1)} copy-done((s32[10,2]{0,1:T(2,128)S(1)}, s32[10,2]{0,1:T(2,128)}, u32[]{:S(2)}) %copy-start.1) | copy-done | bytes 104
  14.0 6.0 %prepare_kernel.1 = (bf16[8,10,64,256]{3,2,1,0:T(8,128)(2,1)S(1)}, f32[48,128]{1,0:T(8,128)S(1)}) custom-call(bf16[160,4096]{1,0:T(8,128)(2,1)} %bitcast.5, s32[2,10]{1,0:T(2,128)S(1)} %bitcast.2, f32[32,128]{1,0:T(8,128)} %mean_at.1, f32[10,32,128]{2,1,0:T(8,128)} %mode_at.1), custom_call_target="tpu_custom_call" | custom-call | flops 134217728 | bytes 4194304 | tf_op jit(solution)/shard_map/prepare_kernel/pallas_call | solution.py:505
  20.1 3.5 %all-to-all-done.slots = f32[32,24,128]{2,1,0:T(8,128)S(1)} async-done(((f32[32,24,128]{2,1,0:T(8,128)}), f32[32,24,128]{2,1,0:T(8,128)S(1)}, u32[]{:S(2)}, u32[]{:S(2)}) %all-to-all-start) | async-done | bytes 393248 | tf_op jit(solution)/shard_map/all_to_all | solution.py:503
  23.6 0.1 send_columns.1.rest_0_.columns_out
  23.8 5.3 %collective-permute-start.1 = (f32[80,128]{1,0:T(8,128)S(1)}, f32[80,128]{1,0:T(8,128)S(1)}, u32[]{:S(2)}, u32[]{:S(2)}) collective-permute-start(f32[80,128]{1,0:T(8,128)S(1)} %send_columns.1.rest_0_.columns_out), channel_id=1, source_target_pairs={{96,1},{0,99},{64,33},{32,67},{80,49},{48,83},{112,17},{16,115},{9... | collective-permute-start | bytes 122888 | tf_op jit(solution)/shard_map/ppermute | solution.py:546
  29.1 0.2 send_rows.1.after.rows_out
  29.3 2.5 %collective-permute-start = (f32[80,128]{1,0:T(8,128)S(1)}, f32[80,128]{1,0:T(8,128)S(1)}, u32[]{:S(2)}, u32[]{:S(2)}) collective-permute-start(f32[80,128]{1,0:T(8,128)S(1)} %send_rows.1.after.rows_out), channel_id=1, source_target_pairs={{16,4},{0,28},{144,132},{128,156},{272,260},{256,284},{400,388},{3... | collective-permute-start | bytes 122888 | tf_op jit(solution)/shard_map/ppermute | solution.py:550
  31.8 0.7 %collective-permute-start.2 = (f32[80,128]{1,0:T(8,128)S(1)}, f32[80,128]{1,0:T(8,128)S(1)}, u32[]{:S(2)}, u32[]{:S(2)}) collective-permute-start(f32[80,128]{1,0:T(8,128)S(1)} %send_again.1.after), channel_id=1, source_target_pairs={{100,5},{4,103},{68,37},{36,71},{84,53},{52,87},{116,21},{20,119},... | collective-permute-start | bytes 122888 | tf_op jit(solution)/shard_map/ppermute | solution.py:554
  32.4 0.0 collective-permute-done.1.also_after.columns_first
  32.5 0.0 copy-done.2
  32.5 4.2 %inner_kernel.1.inner = f32[32,16,128]{2,1,0:T(8,128)S(1)} custom-call(f32[32,24,128]{2,1,0:T(8,128)S(1)} %all-to-all-done.slots, f32[48,128]{1,0:T(8,128)S(1)} %get-tuple-element.7.coefs.rest_0_, bf16[8,10,64,256]{3,2,1,0:T(8,128)(2,1)S(1)} %get-tuple-element.8.weights, s32[2,10]{1,0:T(2,128)S(1)} %bitcast.3, f32[80,128]{1,0:T(8,128)S(1)} %send_again.1.after, ...), custom_call_target="tpu_custom_call" | custom-call | flops 4294967296 | bytes 16777216 | tf_op jit(solution)/shard_map/inner_kernel/pallas_call | solution.py:555
  36.7 0.0 copy-start
  36.7 0.0 collective-permute-done.2.columns_later
  36.7 1.9 %collective-permute-done.rows_in = f32[80,128]{1,0:T(8,128)S(1)} collective-permute-done((f32[80,128]{1,0:T(8,128)S(1)}, f32[80,128]{1,0:T(8,128)S(1)}, u32[]{:S(2)}, u32[]{:S(2)}) %collective-permute-start) | collective-permute-done | bytes 40992 | tf_op jit(solution)/shard_map/ppermute | solution.py:550
  38.6 3.8 %edge_kernel.1 = f32[32,16,128]{2,1,0:T(8,128)} custom-call(f32[80,128]{1,0:T(8,128)S(1)} %send_rows.1.after.rows_out, f32[80,128]{1,0:T(8,128)S(1)} %collective-permute-done.rows_in, f32[80,128]{1,0:T(8,128)S(1)} %send_columns.1.rest_0_.columns_out, f32[80,128]{1,0:T(8,128)S(1)} %collective-permute-done.1.also_after.columns_first, ...), custom_call_target="tpu_custom_call" | custom-call | tf_op jit(solution)/shard_map/edge_kernel/pallas_call | solution.py:562
  42.4 5.5 %all-to-all-start.1 = ((f32[32,16,128]{2,1,0:T(8,128)}), f32[32,16,128]{2,1,0:T(8,128)S(1)}, u32[]{:S(2)}, u32[]{:S(2)}) async-start(f32[32,16,128]{2,1,0:T(8,128)} %edge_kernel.1), calls=%async_computation.1 | async-start | bytes 524288 | tf_op jit(solution)/shard_map/all_to_all | solution.py:576
  49.2 7.7 %all-to-all-done.1.slots = f32[32,16,128]{2,1,0:T(8,128)S(1)} async-done(((f32[32,16,128]{2,1,0:T(8,128)}), f32[32,16,128]{2,1,0:T(8,128)S(1)}, u32[]{:S(2)}, u32[]{:S(2)}) %all-to-all-start.1) | async-done | bytes 262176 | tf_op jit(solution)/shard_map/all_to_all | solution.py:576
  56.9 0.0 copy-done
  56.9 1.2 %finish_kernel.1 = f32[16,32,128]{2,1,0:T(8,128)} custom-call(f32[16,32,128]{2,1,0:T(8,128)S(1)} %copy-done, f32[32,16,128]{2,1,0:T(8,128)S(1)} %all-to-all-done.1.slots, f32[1]{0:T(128)S(6)} %copy.8.lower_bound, f32[1]{0:T(128)S(6)} %copy.9.upper_bound), custom_call_target="tpu_custom_call" | custom-call | tf_op jit(solution)/shard_map/finish_kernel/pallas_call | solution.py:577
  (1 shorter events, 0.0 us)
Async XLA Ops:
  0.0 32.5 %copy-start.2 = (s32[10,2]{0,1:T(2,128)S(1)}, s32[10,2]{0,1:T(2,128)}, u32[]{:S(2)}) copy-start(s32[10,2]{0,1:T(2,128)} %param.11) | copy-start | bytes 244
  2.9 20.7 %all-to-all-start = ((f32[32,24,128]{2,1,0:T(8,128)}), f32[32,24,128]{2,1,0:T(8,128)S(1)}, u32[]{:S(2)}, u32[]{:S(2)}) async-start(f32[32,24,128]{2,1,0:T(8,128)} %pack_kernel.1), calls=%async_computation | async-start | bytes 786432 | tf_op jit(solution)/shard_map/all_to_all | solution.py:503
  13.3 0.7 %copy-start.1 = (s32[10,2]{0,1:T(2,128)S(1)}, s32[10,2]{0,1:T(2,128)}, u32[]{:S(2)}) copy-start(s32[10,2]{0,1:T(2,128)} %param.11) | copy-start | bytes 244
  23.8 8.7 %collective-permute-start.1 = (f32[80,128]{1,0:T(8,128)S(1)}, f32[80,128]{1,0:T(8,128)S(1)}, u32[]{:S(2)}, u32[]{:S(2)}) collective-permute-start(f32[80,128]{1,0:T(8,128)S(1)} %send_columns.1.rest_0_.columns_out), channel_id=1, source_target_pairs={{96,1},{0,99},{64,33},{32,67},{80,49},{48,83},{112,17},{16,115},{9... | collective-permute-start | bytes 122888 | tf_op jit(solution)/shard_map/ppermute | solution.py:546
  29.3 9.3 %collective-permute-start = (f32[80,128]{1,0:T(8,128)S(1)}, f32[80,128]{1,0:T(8,128)S(1)}, u32[]{:S(2)}, u32[]{:S(2)}) collective-permute-start(f32[80,128]{1,0:T(8,128)S(1)} %send_rows.1.after.rows_out), channel_id=1, source_target_pairs={{16,4},{0,28},{144,132},{128,156},{272,260},{256,284},{400,388},{3... | collective-permute-start | bytes 122888 | tf_op jit(solution)/shard_map/ppermute | solution.py:550
  31.8 4.9 %collective-permute-start.2 = (f32[80,128]{1,0:T(8,128)S(1)}, f32[80,128]{1,0:T(8,128)S(1)}, u32[]{:S(2)}, u32[]{:S(2)}) collective-permute-start(f32[80,128]{1,0:T(8,128)S(1)} %send_again.1.after), channel_id=1, source_target_pairs={{100,5},{4,103},{68,37},{36,71},{84,53},{52,87},{116,21},{20,119},... | collective-permute-start | bytes 122888 | tf_op jit(solution)/shard_map/ppermute | solution.py:554
  36.7 20.2 %copy-start = (f32[16,32,128]{2,1,0:T(8,128)S(1)}, f32[16,32,128]{2,1,0:T(8,128)}, u32[]{:S(2)}) copy-start(f32[16,32,128]{2,1,0:T(8,128)} %field.1) | copy-start | bytes 786436
  42.4 14.5 %all-to-all-start.1 = ((f32[32,16,128]{2,1,0:T(8,128)}), f32[32,16,128]{2,1,0:T(8,128)S(1)}, u32[]{:S(2)}, u32[]{:S(2)}) async-start(f32[32,16,128]{2,1,0:T(8,128)} %edge_kernel.1), calls=%async_computation.1 | async-start | bytes 524288 | tf_op jit(solution)/shard_map/all_to_all | solution.py:576

commit v3 on v2

--- a/solution.py
+++ b/solution.py
@@ -10,23 +10,31 @@
 f32 = jnp.float32
 bf16 = jnp.bfloat16
 MODES = 10
+OUTER = ((2, 2), (3, 2), (3, 1), (2, 0), (2, 3), (1, 1), (1, 2), (2, 1))
+INNER = ((0, 2), (0, 1), (0, 0), (1, 0), (3, 0), (3, 3), (0, 3), (1, 3))
 
 
 def block_device(bi, bj):
-    core = (0, 0, 1, 1)[bi]
-    outer = bi in (0, 3)
-    if bj < 4:
-        x, y = (0 if outer else 1), bj
-    else:
-        x, y = (3 if outer else 2), 7 - bj
-    return y * 8 + x * 2 + core
+    x, y = (OUTER if bi in (0, 3) else INNER)[bj]
+    return y * 8 + x * 2 + (0, 0, 1, 1)[bi]
 
 
 def device_block(index):
-    core, x, y = index % 2, (index // 2) % 4, index // 8
-    bi = jnp.where((x == 0) | (x == 3), 3 * core, 1 + core)
-    bj = jnp.where(x < 2, y, 7 - y)
-    return bi, bj
+    core, chip = index % 2, index // 2
+    halves = []
+    for half in range(2):
+        bits = 0
+        for outer, chips in ((1, OUTER), (0, INNER)):
+            for bj, (x, y) in enumerate(chips):
+                if (4 * y + x) // 8 == half:
+                    bits |= (8 * outer + bj) << (4 * ((4 * y + x) % 8))
+        halves.append(bits - 2**32 if bits >= 2**31 else bits)
+    entry = (jnp.where(chip < 8, halves[0], halves[1]) >> (4 * (chip % 8))) & 15
+    bi = jnp.where(entry >= 8, 3 * core, 1 + core)
+    return bi, entry % 8
+
+
+FIRST = block_device(0, 0)
 
 
 def lane_numbers():
@@ -74,8 +82,7 @@
     unit_first, unit_second, unit_third = unit_masks(lane)
     column = lane & 15
     upper, unit_half = column >= 8, column < 4
-    next_place = [(lane >> 4) == 4 + 2 * h for h in range(2)]
-    last_place = [(lane >> 4) == 5 + 2 * h for h in range(2)]
+    first_half = lane < 64
     for copy in copies:
         copy.wait()
     leaving = []
@@ -87,6 +94,14 @@
             blocks.append(swap_chunks(rows, low))
             above.append(field[terms, 8 * bi - 1, :] if bi > 0 else rows[0])
             below.append(field[terms, 8 * bi + 8, :] if bi < 3 else rows[7])
+        beside = [below[0], above[0], below[1], above[1]]
+        for step in (1, 2):
+            for i in range(4):
+                if i & step == 0:
+                    a, b = beside[i], beside[i + step]
+                    beside[i] = jnp.where(low[step], a, roll(b, 16 * step))
+                    beside[i + step] = jnp.where(low[step], roll(a, -16 * step), b)
+        beside = [roll(row, 64) for row in beside] + beside
         for bj in range(8):
             at = block_device(bi, bj)
             units = []
@@ -98,11 +113,7 @@
             row = jnp.where(unit_first, row, roll(row, -8))
             row = jnp.where(unit_second, row, roll(row, -16))
             row = jnp.where(unit_third, row, roll(row, -32))
-            for h in range(2):
-                start = 64 + 32 * h
-                row = jnp.where(next_place[h], roll(below[h], start - 16 * bj), row)
-                row = jnp.where(last_place[h], roll(above[h], start + 16 - 16 * bj), row)
-            slots[at, 16:24, :] = row
+            slots[at, 16:24, :] = jnp.where(first_half, row, beside[bj])
         for bj in range(8):
             at = block_device(bi, bj)
             leaving.append(pltpu.make_async_copy(slots.at[at], target.at[at], left.at[at]))
@@ -112,12 +123,14 @@
 
 
 def prepare_kernel(
-    coupling_at, offsets, mean_at, mode_at, weights, coefs, coupling, pairs, tile, parts, arrived
+    coupling_at, offsets_at, mean_at, mode_at, lower_bound, upper_bound, weights, coefs, scales, coupling, pairs, tile,
+    parts, offsets, arrived,
 ):
     copies = [
         pltpu.make_async_copy(mean_at, tile.at[0], arrived.at[0]),
         pltpu.make_async_copy(mode_at, tile.at[1 : MODES + 1], arrived.at[1]),
         pltpu.make_async_copy(coupling_at, coupling, arrived.at[2]),
+        pltpu.make_async_copy(offsets_at, offsets, arrived.at[3]),
     ]
     for copy in copies:
         copy.start()
@@ -149,6 +162,19 @@
     out_col = lax.broadcasted_iota(jnp.int32, (64, 128), 1)
     pick = jnp.where(out_col & 63 == out_row, 1.0, 0.0).astype(bf16)
     wide = out_col < 64
+    lower_end = jnp.full((8, 128), lower_bound[0], f32)
+    upper_end = jnp.full((8, 128), upper_bound[0], f32)
+    middle = (upper_end + lower_end) * 0.5
+    half_width = (upper_end - lower_end) * 0.5
+    spread_ratio = middle / half_width
+    factor_now = 1.0 / spread_ratio
+    factor_next = 1.0 / (2.0 * spread_ratio - factor_now)
+    residual_scale = 2.0 * factor_next / half_width
+    field_scale = (1.0 + factor_next * factor_now) / middle + residual_scale
+    applied_scale = residual_scale / middle
+    scales[0:8, :] = field_scale
+    scales[8:16, :] = applied_scale
+    copies[3].wait()
     copies[2].wait()
 
     def one_mode(k, carry):
@@ -172,7 +198,7 @@
             weights[d, k, :, 128:256] = turned.astype(bf16)
         return carry
 
-    lax.fori_loop(0, MODES, one_mode, 0, unroll=2)
+    lax.fori_loop(0, MODES, one_mode, 0, unroll=5)
 
 
 def send_kernel(along_rows, slots, coefs, *rest):
@@ -206,10 +232,16 @@
     sent[...] = columns_out[...]
 
 
-def inner_kernel(slots, coefs, weights, offsets_at, after, also_after, out, faces, spread, offsets, arrived):
-    copy = pltpu.make_async_copy(offsets_at, offsets, arrived.at[0])
-    copy.start()
-    inner_operator(slots, coefs, weights, offsets, copy, out, faces, spread)
+def inner_kernel(first, slots, coefs, weights, offsets_at, *rest):
+    out, faces, spread, offsets, arrived = rest[-5:]
+    bi, bj = device_block(lax.axis_index("chaos"))
+    before = (lax.axis_index("sx") == 0) & (bi == 0) & (bj > 0) & (bj < 7)
+
+    @pl.when(before == first)
+    def _():
+        copy = pltpu.make_async_copy(offsets_at, offsets, arrived.at[0])
+        copy.start()
+        inner_operator(slots, coefs, weights, offsets, copy, out, faces, spread)
 
 
 def inner_operator(slots, coefs, weights, offsets, offsets_copy, out, faces, spread):
@@ -292,13 +324,7 @@
     lax.fori_loop(0, 8, one_block, 0, unroll=8)
 
 
-def wait_blocks(source, target, left):
-    for d in range(8):
-        part = slice(4 * d, 4 * d + 4)
-        pltpu.make_async_copy(source.at[part], target.at[part], left.at[d]).wait()
-
-
-def edge_kernel(rows_out, rows_in, columns_out, columns_first, columns_later, weights, offsets_at, inner, target, steps, spread, columns_in, out, left,
+def edge_kernel(rows_out, rows_in, columns_out, columns_first, columns_later, weights, offsets_at, inner, source, out, field, steps, spread, columns_in,
     offsets, arrived,
 ):
     bi, bj = device_block(lax.axis_index("chaos"))
@@ -306,12 +332,13 @@
     on_column = (bj == 0) | (bj == 7)
     offsets_copy = pltpu.make_async_copy(offsets_at, offsets, arrived.at[0])
     offsets_copy.start()
+    field_copy = pltpu.make_async_copy(source, field, arrived.at[1])
+    field_copy.start()
 
     @pl.when(jnp.logical_not(on_row | on_column))
     def _():
-        copy = pltpu.make_async_copy(inner, target, left.at[0])
-        copy.start()
-        copy.wait()
+        out[: 32 - FIRST] = inner[FIRST:]
+        out[32 - FIRST :] = inner[:FIRST]
         offsets_copy.wait()
 
     early = lax.axis_index("sx") == 0
@@ -327,15 +354,16 @@
     @pl.when(on_row | on_column)
     def _():
         edge_faces(
-            bi, bj, on_row, on_column, rows_out, rows_in, columns_out, columns_in, weights, offsets, inner, out, steps, spread, target, left,
+            bi, bj, on_row, on_column, rows_out, rows_in, columns_out, columns_in, weights, offsets, inner, out, steps, spread,
             offsets_copy,
         )
-        wait_blocks(out, target, left)
+
+    field_copy.wait()
 
 
 def edge_faces(
     bi, bj, on_row, on_column, rows_out, rows_in, columns_out, columns_in, weights, offsets, inner, out, steps, spread,
-    target, left, offsets_copy,
+    offsets_copy,
 ):
     lane = lane_numbers()
     column = lane & 15
@@ -416,31 +444,22 @@
         middle = rest.astype(bf16)
         low = (rest - middle.astype(f32)).astype(bf16)
         placed = jnp.dot(jnp.concatenate([high, middle, low], axis=1), place, preferred_element_type=f32)
+        to = lax.rem(4 * d + 32 - FIRST, 32)
         for part in range(4):
-            out[4 * d + part] = inner[4 * d + part] + placed[16 * part : 16 * part + 16]
-        pltpu.make_async_copy(out.at[pl.ds(4 * d, 4)], target.at[pl.ds(4 * d, 4)], left.at[d]).start()
+            out[to + part] = inner[4 * d + part] + placed[16 * part : 16 * part + 16]
         return carry
 
     lax.fori_loop(0, 8, one_block, 0, unroll=8)
 
 
-def finish_kernel(field, slots, lower_bound, upper_bound, target, out, left):
+def finish_kernel(field, slots, scales, target, out, left):
     low = chunk_masks(lane_numbers())
-    lower_end = jnp.full((8, 128), lower_bound[0], f32)
-    upper_end = jnp.full((8, 128), upper_bound[0], f32)
-    middle = (upper_end + lower_end) * 0.5
-    half_width = (upper_end - lower_end) * 0.5
-    spread_ratio = middle / half_width
-    factor_now = 1.0 / spread_ratio
-    factor_next = 1.0 / (2.0 * spread_ratio - factor_now)
-    residual_scale = 2.0 * factor_next / half_width
-    field_scale = (1.0 + factor_next * factor_now) / middle + residual_scale
-    applied_scale = residual_scale / middle
+    field_scale, applied_scale = scales[0:8, :], scales[8:16, :]
     copies = []
     for bi in range(4):
         for h in range(2):
             terms = slice(8 * h, 8 * h + 8)
-            rows = swap_chunks([slots[block_device(bi, bj), terms, :] for bj in range(8)], low)
+            rows = swap_chunks([slots[(block_device(bi, bj) - FIRST) % 32, terms, :] for bj in range(8)], low)
             for i in range(8):
                 at = 8 * bi + i
                 out[terms, at, :] = field_scale * field[terms, at, :] - applied_scale * rows[i]
@@ -501,21 +520,22 @@
         limit=32,
     )(from_hbm(right_side))
     held = lax.all_to_all(slots, "chaos", 0, 0, tiled=True)
-    offsets = offsets.T
-    weights, coefs = call(
+    offsets = from_hbm(offsets.T)
+    weights, coefs, scales = call(
         prepare_kernel,
-        [in_hbm(), in_smem(), in_hbm(), in_hbm()],
-        (pltpu.VMEM((8, MODES, 64, 256), bf16), pltpu.VMEM((48, 128), f32)),
+        [in_hbm()] * 4 + [in_smem()] * 2,
+        (pltpu.VMEM((8, MODES, 64, 256), bf16), pltpu.VMEM((48, 128), f32), pltpu.VMEM((16, 128), f32)),
         [
             pltpu.VMEM((16 * MODES, 4096), bf16),
             pltpu.VMEM((512 * MODES, 128), f32),
             pltpu.VMEM((16, 32, 128), f32),
             pltpu.VMEM((8, 8, 128), f32),
-            pltpu.SemaphoreType.DMA((3,)),
+            pltpu.SMEM((2, MODES), jnp.int32),
+            pltpu.SemaphoreType.DMA((4,)),
         ],
         pl.CostEstimate(flops=2**27, bytes_accessed=2**22, transcendentals=0),
         limit=32,
-    )(from_hbm(coupling.reshape(16 * MODES, 4096)), offsets, from_hbm(mean_coef), from_hbm(mode_coef))
+    )(from_hbm(coupling.reshape(16 * MODES, 4096)), offsets, from_hbm(mean_coef), from_hbm(mode_coef), lower_bound, upper_bound)
     def index(device, sx, sy):
         return (device * 4 + sx % 4) * 4 + sy % 4
 
@@ -544,43 +564,54 @@
         functools.partial(send_kernel, False), [in_vmem()] * 2 + [in_any()], message, name="send_columns"
     )(held, coefs, coefs)
     columns_first = lax.ppermute(columns_out, axes, early_pairs)
+    inner = call(
+        functools.partial(inner_kernel, True),
+        [in_vmem()] * 3 + [in_hbm()] + [in_any()],
+        inner_shape,
+        scratch,
+        inner_cost,
+        name="inner_before",
+    )(held, coefs, weights, offsets, columns_out)
     rows_out = call(
         functools.partial(send_kernel, True), [in_vmem()] * 2 + [in_any()], message, name="send_rows"
-    )(held, coefs, columns_out)
+    )(held, coefs, inner)
     rows_in = lax.ppermute(rows_out, axes, row_pairs)
     columns_again = call(again_kernel, [in_vmem(), in_any()], message, name="send_again")(
         columns_out, rows_out
     )
     columns_later = lax.ppermute(columns_again, axes, late_pairs)
     inner = call(
-        inner_kernel,
-        [in_vmem()] * 3 + [in_any()] * 3,
+        functools.partial(inner_kernel, False),
+        [in_vmem()] * 3 + [in_hbm(), in_vmem()] + [in_any()] * 2,
         inner_shape,
         scratch,
         inner_cost,
-    )(held, coefs, weights, offsets, columns_again, columns_first)
-    applied = call(
+        aliases={4: 0},
+        name="inner_after",
+    )(held, coefs, weights, offsets, inner, columns_again, columns_first)
+    applied, field = call(
         edge_kernel,
-        [in_vmem()] * 6 + [in_any(), in_vmem()],
-        pltpu.HBM((32, 16, 128), f32),
+        [in_vmem()] * 6 + [in_hbm(), in_vmem(), in_hbm()],
+        (pltpu.VMEM((32, 16, 128), f32), pltpu.VMEM(right_side.shape, f32)),
         [
             pltpu.VMEM((128 + 512, 128), f32),
             pltpu.VMEM((512 * MODES, 128), bf16),
             pltpu.VMEM((80, 128), f32),
-            pltpu.VMEM((32, 16, 128), f32),
-            pltpu.SemaphoreType.DMA((8,)),
-        ]
-        + offsets_scratch,
-        out_specs=in_hbm(),
-    )(rows_out, rows_in, columns_out, columns_first, columns_later, weights, offsets, inner)
-    returned = lax.all_to_all(applied, "chaos", 0, 0, tiled=True)
+            pltpu.SMEM((2, MODES), jnp.int32),
+            pltpu.SemaphoreType.DMA((2,)),
+        ],
+    )(
+        rows_out, rows_in, columns_out, columns_first, columns_later, weights, offsets, inner, from_hbm(right_side)
+    )
+    turned = [[(FIRST + i) % 32 for i in range(32)]]
+    returned = lax.all_to_all(applied, "chaos", 0, 0, tiled=True, axis_index_groups=turned)
     return call(
         finish_kernel,
-        [in_vmem()] * 2 + [in_smem()] * 2,
+        [in_vmem()] * 3,
         pltpu.HBM(right_side.shape, f32),
         [pltpu.VMEM(right_side.shape, f32), pltpu.SemaphoreType.DMA((4,))],
         out_specs=in_hbm(),
-    )(right_side, returned, lower_bound, upper_bound)
+    )(field, returned, scales)
 
 
 def solution(mesh):

time: 58.6 us -> 53.8 us (0.918)
  blocking collectives: 0 us -> 21 us
  starting transfers between devices: 24.4 us -> 12.4 us
  waiting for transfers between devices: 13.1 us -> 3.63 us
  Pallas kernels: 18.5 us -> 14.9 us
  local copies, waits for them, and re-layouts: 0.68 us -> 0 us
    all_to_all x0 -> x1, blocking collectives: none -> 21 us  [per_device(): lax.all_to_all(applied, 'chaos', 0, 0, tiled=True, axis_index_groups=turned)]
    all_to_all x1 -> x0, waiting for transfers between devices: 7.66 us -> none  [per_device(): returned = lax.all_to_all(applied, 'chaos', 0, 0, tiled=True)]
    all_to_all x1 -> x0, starting transfers between devices: 5.51 us -> none  [per_device(): returned = lax.all_to_all(applied, 'chaos', 0, 0, tiled=True)]
    ppermute x1, starting transfers between devices: 5.31 us -> 0.66 us  [per_device(): columns_first = lax.ppermute(columns_out, axes, early_pairs)]
    pallas_call x4 -> x5, Pallas kernels: 15.2 us -> 11.8 us  [the longest x1 5.36 us: per_device(): call(prepare_kernel, [in_hbm()] * 4 + [in_smem()] * 2, (pltpu.VMEM((8, MO...]
    ppermute x1, waiting for transfers between devices: 1.93 us -> 0.01 us  [per_device(): rows_in = lax.ppermute(rows_out, axes, row_pairs)]
    ppermute x1, starting transfers between devices: 2.49 us -> 0.66 us  [per_device(): rows_in = lax.ppermute(rows_out, axes, row_pairs)]
    unnamed x6 -> x0, local copies, waits for them, and re-layouts: 0.68 us -> none
  transfers between devices with their start and end apart: 5 -> 4, of which waited for: 3 -> 1; matrix products, arithmetic and copies ran while one was open for 0% -> 0% of each run, Pallas kernels for 18% -> 18%
where the time goes in v3:
time: 53.8 us; the launch traced here: 53.4 us
  blocking collectives  21 us (39%)
  Pallas kernels  14.9 us (28%)
  starting transfers between devices  12.4 us (23%)
  waiting for transfers between devices  3.63 us (7%)
  between operations  1.4 us (3%)
    all_to_all x1, blocking collectives, per_device(): lax.all_to_all(applied, 'chaos', 0, 0, tiled=True, axis_index_groups=turned)  21 us
    all_to_all x1, starting transfers between devices, per_device(): held = lax.all_to_all(slots, 'chaos', 0, 0, tiled=True)  10.4 us
    pallas_call x1, Pallas kernels, per_device(): call(prepare_kernel, [in_hbm()] * 4 + [in_smem()] * 2, (pltpu.VMEM((8, MO...  5.36 us
    pallas_call x1, Pallas kernels, per_device(): call(functools.partial(inner_kernel, False), [in_vmem()] * 3 + [in_hbm(),...  4.22 us
    all_to_all x1, waiting for transfers between devices, per_device(): held = lax.all_to_all(slots, 'chaos', 0, 0, tiled=True)  3.62 us
    pallas_call x1, Pallas kernels, per_device(): call(pack_kernel, [in_hbm()], pltpu.HBM((32, 24, 128), f32), [pltpu.VMEM(...  2.84 us
    pallas_call x1, Pallas kernels, per_device(): call(finish_kernel, [in_vmem()] * 3, pltpu.HBM(right_side.shape, f32), [p...  1.17 us
  transfers between devices with their start and end apart: 4, of which 1 were waited for; matrix products, arithmetic and copies ran while one was open for 0% of the time, Pallas kernels for 18%

profile of v3, /device:TPU:1, one launch (start us, length us, event | category | flops | bytes accessed | tf_op | source)
XLA Modules:
  0.0 53.4 jit_solution(5023326570302539002)
XLA Ops:
  0.0 2.8 %pack_kernel.1 = f32[32,24,128]{2,1,0:T(8,128)} custom-call(f32[16,32,128]{2,1,0:T(8,128)} %source.3), custom_call_target="tpu_custom_call" | custom-call | tf_op jit(solution)/shard_map/pack_kernel/pallas_call | solution.py:509
  2.8 10.4 %all-to-all-start = ((f32[32,24,128]{2,1,0:T(8,128)}), f32[32,24,128]{2,1,0:T(8,128)S(1)}, u32[]{:S(2)}, u32[]{:S(2)}) async-start(f32[32,24,128]{2,1,0:T(8,128)} %pack_kernel.1), calls=%async_computation | async-start | bytes 786432 | tf_op jit(solution)/shard_map/all_to_all | solution.py:522
  14.6 5.4 %prepare_kernel.1 = (bf16[8,10,64,256]{3,2,1,0:T(8,128)(2,1)S(1)}, f32[48,128]{1,0:T(8,128)S(1)}, f32[16,128]{1,0:T(8,128)S(1)}) custom-call(bf16[160,4096]{1,0:T(8,128)(2,1)} %bitcast.2, s32[2,10]{1,0:T(2,128)} %bitcast.3, f32[32,128]{1,0:T(8,128)} %mean_at.1, f32[10,32,128]{2,1,0:T(8,128)} %mode_at.1, f32[1]{0:T(128)S(6)} %copy.10.lower_bound, ...), custom_call_target="tpu_custom_call" | custom-call | flops 134217728 | bytes 4194304 | tf_op jit(solution)/shard_map/prepare_kernel/pallas_call | solution.py:524
  19.9 3.6 %all-to-all-done.slots = f32[32,24,128]{2,1,0:T(8,128)S(1)} async-done(((f32[32,24,128]{2,1,0:T(8,128)}), f32[32,24,128]{2,1,0:T(8,128)S(1)}, u32[]{:S(2)}, u32[]{:S(2)}) %all-to-all-start) | async-done | bytes 393248 | tf_op jit(solution)/shard_map/all_to_all | solution.py:522
  23.6 0.2 send_columns.1.rest_0_.columns_out
  23.7 0.7 %collective-permute-start.1 = (f32[80,128]{1,0:T(8,128)S(1)}, f32[80,128]{1,0:T(8,128)S(1)}, u32[]{:S(2)}, u32[]{:S(2)}) collective-permute-start(f32[80,128]{1,0:T(8,128)S(1)} %send_columns.1.rest_0_.columns_out), channel_id=1, source_target_pairs={{192,321},{320,195},{416,257},{256,419},{432,273},{272,435},{208,3... | collective-permute-start | bytes 122888 | tf_op jit(solution)/shard_map/ppermute | solution.py:566
  24.4 0.2 send_rows.1.after.rows_out
  24.6 0.7 %collective-permute-start = (f32[80,128]{1,0:T(8,128)S(1)}, f32[80,128]{1,0:T(8,128)S(1)}, u32[]{:S(2)}, u32[]{:S(2)}) collective-permute-start(f32[80,128]{1,0:T(8,128)S(1)} %send_rows.1.after.rows_out), channel_id=1, source_target_pairs={{336,324},{320,348},{368,356},{352,380},{240,228},{224,252},{80,68... | collective-permute-start | bytes 122888 | tf_op jit(solution)/shard_map/ppermute | solution.py:578
  25.3 0.7 %collective-permute-start.2 = (f32[80,128]{1,0:T(8,128)S(1)}, f32[80,128]{1,0:T(8,128)S(1)}, u32[]{:S(2)}, u32[]{:S(2)}) collective-permute-start(f32[80,128]{1,0:T(8,128)S(1)} %send_again.1.rest_1_), channel_id=1, source_target_pairs={{196,325},{324,199},{420,261},{260,423},{436,277},{276,439},{212,3... | collective-permute-start | bytes 122888 | tf_op jit(solution)/shard_map/ppermute | solution.py:582
  26.0 0.0 collective-permute-done.1.rest_2_.columns_first
  26.0 4.2 %inner_after.1.inner = f32[32,16,128]{2,1,0:T(8,128)S(1)} custom-call(f32[32,24,128]{2,1,0:T(8,128)S(1)} %all-to-all-done.slots, f32[48,128]{1,0:T(8,128)S(1)} %get-tuple-element.10.coefs.rest_0_, bf16[8,10,64,256]{3,2,1,0:T(8,128)(2,1)S(1)} %get-tuple-element.11.weights, s32[2,10]{1,0:T(2,128)} %bitcast.5, ...), custom_call_target="tpu_custom_call", output_to_operand_aliasing={{}: (4, {})} | custom-call | flops 4294967296 | bytes 16777216 | tf_op jit(solution)/shard_map/inner_after/pallas_call | solution.py:583
  30.2 0.0 collective-permute-done.2.columns_later
  30.2 0.0 collective-permute-done.rows_in
  30.2 1.0 %edge_kernel.1 = (f32[32,16,128]{2,1,0:T(8,128)S(1)}, f32[16,32,128]{2,1,0:T(8,128)S(1)}) custom-call(f32[80,128]{1,0:T(8,128)S(1)} %send_rows.1.after.rows_out, f32[80,128]{1,0:T(8,128)S(1)} %collective-permute-done.rows_in, f32[80,128]{1,0:T(8,128)S(1)} %send_columns.1.rest_0_.columns_out, f32[80,128]{1,0:T(8,128)S(1)} %collective-permute-done.1.rest_2_.columns_first, ...), custom_call_target="tpu_custom_call" | custom-call | tf_op jit(solution)/shard_map/edge_kernel/pallas_call | solution.py:592
  31.2 21.0 %all_to_all.10.slots = f32[32,16,128]{2,1,0:T(8,128)S(1)} all-to-all(f32[32,16,128]{2,1,0:T(8,128)S(1)} %get-tuple-element.13), channel_id=1, replica_groups={{320,336,352,368,384,400,416,432,448,464,480,496,0,16,32,48,64,80,96,11..., dimensions={0} | all-to-all | bytes 524288 | tf_op jit(solution)/shard_map/all_to_all | solution.py:607
  52.2 1.2 %finish_kernel.1 = f32[16,32,128]{2,1,0:T(8,128)} custom-call(f32[16,32,128]{2,1,0:T(8,128)S(1)} %get-tuple-element.12.field, f32[32,16,128]{2,1,0:T(8,128)S(1)} %all_to_all.10.slots, f32[16,128]{1,0:T(8,128)S(1)} %get-tuple-element.14.scales), custom_call_target="tpu_custom_call" | custom-call | tf_op jit(solution)/shard_map/finish_kernel/pallas_call | solution.py:608
  (2 shorter events, 0.0 us)
Async XLA Ops:
  2.8 20.7 %all-to-all-start = ((f32[32,24,128]{2,1,0:T(8,128)}), f32[32,24,128]{2,1,0:T(8,128)S(1)}, u32[]{:S(2)}, u32[]{:S(2)}) async-start(f32[32,24,128]{2,1,0:T(8,128)} %pack_kernel.1), calls=%async_computation | async-start | bytes 786432 | tf_op jit(solution)/shard_map/all_to_all | solution.py:522
  23.7 2.2 %collective-permute-start.1 = (f32[80,128]{1,0:T(8,128)S(1)}, f32[80,128]{1,0:T(8,128)S(1)}, u32[]{:S(2)}, u32[]{:S(2)}) collective-permute-start(f32[80,128]{1,0:T(8,128)S(1)} %send_columns.1.rest_0_.columns_out), channel_id=1, source_target_pairs={{192,321},{320,195},{416,257},{256,419},{432,273},{272,435},{208,3... | collective-permute-start | bytes 122888 | tf_op jit(solution)/shard_map/ppermute | solution.py:566
  24.6 5.6 %collective-permute-start = (f32[80,128]{1,0:T(8,128)S(1)}, f32[80,128]{1,0:T(8,128)S(1)}, u32[]{:S(2)}, u32[]{:S(2)}) collective-permute-start(f32[80,128]{1,0:T(8,128)S(1)} %send_rows.1.after.rows_out), channel_id=1, source_target_pairs={{336,324},{320,348},{368,356},{352,380},{240,228},{224,252},{80,68... | collective-permute-start | bytes 122888 | tf_op jit(solution)/shard_map/ppermute | solution.py:578
  25.3 4.9 %collective-permute-start.2 = (f32[80,128]{1,0:T(8,128)S(1)}, f32[80,128]{1,0:T(8,128)S(1)}, u32[]{:S(2)}, u32[]{:S(2)}) collective-permute-start(f32[80,128]{1,0:T(8,128)S(1)} %send_again.1.rest_1_), channel_id=1, source_target_pairs={{196,325},{324,199},{420,261},{260,423},{436,277},{276,439},{212,3... | collective-permute-start | bytes 122888 | tf_op jit(solution)/shard_map/ppermute | solution.py:582

commit v4 on v3

--- a/solution.py
+++ b/solution.py
@@ -527,7 +527,7 @@
         (pltpu.VMEM((8, MODES, 64, 256), bf16), pltpu.VMEM((48, 128), f32), pltpu.VMEM((16, 128), f32)),
         [
             pltpu.VMEM((16 * MODES, 4096), bf16),
-            pltpu.VMEM((512 * MODES, 128), f32),
+            pltpu.VMEM((512 * MODES + 64, 128), f32),
             pltpu.VMEM((16, 32, 128), f32),
             pltpu.VMEM((8, 8, 128), f32),
             pltpu.SMEM((2, MODES), jnp.int32),

time: 53.8 us -> 53.8 us (level)
  no operation moved by 1% of the time
where the time goes in v4:
time: 53.8 us; the launch traced here: 53.4 us
  blocking collectives  21 us (39%)
  Pallas kernels  14.9 us (28%)
  starting transfers between devices  12.4 us (23%)
  waiting for transfers between devices  3.63 us (7%)
  between operations  1.4 us (3%)
    all_to_all x1, blocking collectives, per_device(): lax.all_to_all(applied, 'chaos', 0, 0, tiled=True, axis_index_groups=turned)  21 us
    all_to_all x1, starting transfers between devices, per_device(): held = lax.all_to_all(slots, 'chaos', 0, 0, tiled=True)  10.4 us
    pallas_call x1, Pallas kernels, per_device(): call(prepare_kernel, [in_hbm()] * 4 + [in_smem()] * 2, (pltpu.VMEM((8, MO...  5.36 us
    pallas_call x1, Pallas kernels, per_device(): call(functools.partial(inner_kernel, False), [in_vmem()] * 3 + [in_hbm(),...  4.22 us
    all_to_all x1, waiting for transfers between devices, per_device(): held = lax.all_to_all(slots, 'chaos', 0, 0, tiled=True)  3.62 us
    pallas_call x1, Pallas kernels, per_device(): call(pack_kernel, [in_hbm()], pltpu.HBM((32, 24, 128), f32), [pltpu.VMEM(...  2.84 us
    pallas_call x1, Pallas kernels, per_device(): call(finish_kernel, [in_vmem()] * 3, pltpu.HBM(right_side.shape, f32), [p...  1.17 us
  transfers between devices with their start and end apart: 4, of which 1 were waited for; matrix products, arithmetic and copies ran while one was open for 0% of the time, Pallas kernels for 18%

profile of v4, /device:TPU:1, one launch (start us, length us, event | category | flops | bytes accessed | tf_op | source)
XLA Modules:
  0.0 53.4 jit_solution(10702707016780490491)
XLA Ops:
  0.0 2.8 %pack_kernel.1 = f32[32,24,128]{2,1,0:T(8,128)} custom-call(f32[16,32,128]{2,1,0:T(8,128)} %source.3), custom_call_target="tpu_custom_call" | custom-call | tf_op jit(solution)/shard_map/pack_kernel/pallas_call | solution.py:509
  2.8 10.4 %all-to-all-start = ((f32[32,24,128]{2,1,0:T(8,128)}), f32[32,24,128]{2,1,0:T(8,128)S(1)}, u32[]{:S(2)}, u32[]{:S(2)}) async-start(f32[32,24,128]{2,1,0:T(8,128)} %pack_kernel.1), calls=%async_computation | async-start | bytes 786432 | tf_op jit(solution)/shard_map/all_to_all | solution.py:522
  14.6 5.4 %prepare_kernel.1 = (bf16[8,10,64,256]{3,2,1,0:T(8,128)(2,1)S(1)}, f32[48,128]{1,0:T(8,128)S(1)}, f32[16,128]{1,0:T(8,128)S(1)}) custom-call(bf16[160,4096]{1,0:T(8,128)(2,1)} %bitcast.2, s32[2,10]{1,0:T(2,128)} %bitcast.3, f32[32,128]{1,0:T(8,128)} %mean_at.1, f32[10,32,128]{2,1,0:T(8,128)} %mode_at.1, f32[1]{0:T(128)S(6)} %copy.10.lower_bound, ...), custom_call_target="tpu_custom_call" | custom-call | flops 134217728 | bytes 4194304 | tf_op jit(solution)/shard_map/prepare_kernel/pallas_call | solution.py:524
  19.9 3.6 %all-to-all-done.slots = f32[32,24,128]{2,1,0:T(8,128)S(1)} async-done(((f32[32,24,128]{2,1,0:T(8,128)}), f32[32,24,128]{2,1,0:T(8,128)S(1)}, u32[]{:S(2)}, u32[]{:S(2)}) %all-to-all-start) | async-done | bytes 393248 | tf_op jit(solution)/shard_map/all_to_all | solution.py:522
  23.6 0.2 send_columns.1.rest_0_.columns_out
  23.7 0.7 %collective-permute-start.1 = (f32[80,128]{1,0:T(8,128)S(1)}, f32[80,128]{1,0:T(8,128)S(1)}, u32[]{:S(2)}, u32[]{:S(2)}) collective-permute-start(f32[80,128]{1,0:T(8,128)S(1)} %send_columns.1.rest_0_.columns_out), channel_id=1, source_target_pairs={{192,321},{320,195},{416,257},{256,419},{432,273},{272,435},{208,3... | collective-permute-start | bytes 122888 | tf_op jit(solution)/shard_map/ppermute | solution.py:566
  24.4 0.2 send_rows.1.after.rows_out
  24.6 0.7 %collective-permute-start = (f32[80,128]{1,0:T(8,128)S(1)}, f32[80,128]{1,0:T(8,128)S(1)}, u32[]{:S(2)}, u32[]{:S(2)}) collective-permute-start(f32[80,128]{1,0:T(8,128)S(1)} %send_rows.1.after.rows_out), channel_id=1, source_target_pairs={{336,324},{320,348},{368,356},{352,380},{240,228},{224,252},{80,68... | collective-permute-start | bytes 122888 | tf_op jit(solution)/shard_map/ppermute | solution.py:578
  25.3 0.7 %collective-permute-start.2 = (f32[80,128]{1,0:T(8,128)S(1)}, f32[80,128]{1,0:T(8,128)S(1)}, u32[]{:S(2)}, u32[]{:S(2)}) collective-permute-start(f32[80,128]{1,0:T(8,128)S(1)} %send_again.1.rest_1_), channel_id=1, source_target_pairs={{196,325},{324,199},{420,261},{260,423},{436,277},{276,439},{212,3... | collective-permute-start | bytes 122888 | tf_op jit(solution)/shard_map/ppermute | solution.py:582
  26.0 0.0 collective-permute-done.1.rest_2_.columns_first
  26.0 4.2 %inner_after.1.inner = f32[32,16,128]{2,1,0:T(8,128)S(1)} custom-call(f32[32,24,128]{2,1,0:T(8,128)S(1)} %all-to-all-done.slots, f32[48,128]{1,0:T(8,128)S(1)} %get-tuple-element.10.coefs.rest_0_, bf16[8,10,64,256]{3,2,1,0:T(8,128)(2,1)S(1)} %get-tuple-element.11.weights, s32[2,10]{1,0:T(2,128)} %bitcast.5, ...), custom_call_target="tpu_custom_call", output_to_operand_aliasing={{}: (4, {})} | custom-call | flops 4294967296 | bytes 16777216 | tf_op jit(solution)/shard_map/inner_after/pallas_call | solution.py:583
  30.2 0.0 collective-permute-done.2.columns_later
  30.2 0.0 collective-permute-done.rows_in
  30.2 1.0 %edge_kernel.1 = (f32[32,16,128]{2,1,0:T(8,128)S(1)}, f32[16,32,128]{2,1,0:T(8,128)S(1)}) custom-call(f32[80,128]{1,0:T(8,128)S(1)} %send_rows.1.after.rows_out, f32[80,128]{1,0:T(8,128)S(1)} %collective-permute-done.rows_in, f32[80,128]{1,0:T(8,128)S(1)} %send_columns.1.rest_0_.columns_out, f32[80,128]{1,0:T(8,128)S(1)} %collective-permute-done.1.rest_2_.columns_first, ...), custom_call_target="tpu_custom_call" | custom-call | tf_op jit(solution)/shard_map/edge_kernel/pallas_call | solution.py:592
  31.2 21.0 %all_to_all.10.slots = f32[32,16,128]{2,1,0:T(8,128)S(1)} all-to-all(f32[32,16,128]{2,1,0:T(8,128)S(1)} %get-tuple-element.13), channel_id=1, replica_groups={{320,336,352,368,384,400,416,432,448,464,480,496,0,16,32,48,64,80,96,11..., dimensions={0} | all-to-all | bytes 524288 | tf_op jit(solution)/shard_map/all_to_all | solution.py:607
  52.2 1.2 %finish_kernel.1 = f32[16,32,128]{2,1,0:T(8,128)} custom-call(f32[16,32,128]{2,1,0:T(8,128)S(1)} %get-tuple-element.12.field, f32[32,16,128]{2,1,0:T(8,128)S(1)} %all_to_all.10.slots, f32[16,128]{1,0:T(8,128)S(1)} %get-tuple-element.14.scales), custom_call_target="tpu_custom_call" | custom-call | tf_op jit(solution)/shard_map/finish_kernel/pallas_call | solution.py:608
  (2 shorter events, 0.0 us)
Async XLA Ops:
  2.8 20.7 %all-to-all-start = ((f32[32,24,128]{2,1,0:T(8,128)}), f32[32,24,128]{2,1,0:T(8,128)S(1)}, u32[]{:S(2)}, u32[]{:S(2)}) async-start(f32[32,24,128]{2,1,0:T(8,128)} %pack_kernel.1), calls=%async_computation | async-start | bytes 786432 | tf_op jit(solution)/shard_map/all_to_all | solution.py:522
  23.7 2.2 %collective-permute-start.1 = (f32[80,128]{1,0:T(8,128)S(1)}, f32[80,128]{1,0:T(8,128)S(1)}, u32[]{:S(2)}, u32[]{:S(2)}) collective-permute-start(f32[80,128]{1,0:T(8,128)S(1)} %send_columns.1.rest_0_.columns_out), channel_id=1, source_target_pairs={{192,321},{320,195},{416,257},{256,419},{432,273},{272,435},{208,3... | collective-permute-start | bytes 122888 | tf_op jit(solution)/shard_map/ppermute | solution.py:566
  24.6 5.6 %collective-permute-start = (f32[80,128]{1,0:T(8,128)S(1)}, f32[80,128]{1,0:T(8,128)S(1)}, u32[]{:S(2)}, u32[]{:S(2)}) collective-permute-start(f32[80,128]{1,0:T(8,128)S(1)} %send_rows.1.after.rows_out), channel_id=1, source_target_pairs={{336,324},{320,348},{368,356},{352,380},{240,228},{224,252},{80,68... | collective-permute-start | bytes 122888 | tf_op jit(solution)/shard_map/ppermute | solution.py:578
  25.3 4.9 %collective-permute-start.2 = (f32[80,128]{1,0:T(8,128)S(1)}, f32[80,128]{1,0:T(8,128)S(1)}, u32[]{:S(2)}, u32[]{:S(2)}) collective-permute-start(f32[80,128]{1,0:T(8,128)S(1)} %send_again.1.rest_1_), channel_id=1, source_target_pairs={{196,325},{324,199},{420,261},{260,423},{436,277},{276,439},{212,3... | collective-permute-start | bytes 122888 | tf_op jit(solution)/shard_map/ppermute | solution.py:582

commit v5 on v4

--- a/solution.py
+++ b/solution.py
@@ -114,10 +114,10 @@
             row = jnp.where(unit_second, row, roll(row, -16))
             row = jnp.where(unit_third, row, roll(row, -32))
             slots[at, 16:24, :] = jnp.where(first_half, row, beside[bj])
-        for bj in range(8):
-            at = block_device(bi, bj)
-            leaving.append(pltpu.make_async_copy(slots.at[at], target.at[at], left.at[at]))
-            leaving[-1].start()
+    for part in range(8):
+        at = slice(4 * part, 4 * part + 4)
+        leaving.append(pltpu.make_async_copy(slots.at[at], target.at[at], left.at[part]))
+        leaving[-1].start()
     for copy in leaving:
         copy.wait()
 
@@ -514,7 +514,7 @@
             pltpu.VMEM((16, 32, 128), f32),
             pltpu.VMEM((32, 24, 128), f32),
             pltpu.SemaphoreType.DMA((4,)),
-            pltpu.SemaphoreType.DMA((32,)),
+            pltpu.SemaphoreType.DMA((8,)),
         ],
         out_specs=in_hbm(),
         limit=32,

time: 53.8 us -> 53.6 us (level)
  no operation moved by 1% of the time
where the time goes in v5:
time: 53.6 us; the launch traced here: 53.2 us
  blocking collectives  21 us (39%)
  Pallas kernels  14.7 us (27%)
  starting transfers between devices  12.4 us (23%)
  waiting for transfers between devices  3.63 us (7%)
  between operations  1.4 us (3%)
    all_to_all x1, blocking collectives, per_device(): lax.all_to_all(applied, 'chaos', 0, 0, tiled=True, axis_index_groups=turned)  21 us
    all_to_all x1, starting transfers between devices, per_device(): held = lax.all_to_all(slots, 'chaos', 0, 0, tiled=True)  10.4 us
    pallas_call x1, Pallas kernels, per_device(): call(prepare_kernel, [in_hbm()] * 4 + [in_smem()] * 2, (pltpu.VMEM((8, MO...  5.36 us
    pallas_call x1, Pallas kernels, per_device(): call(functools.partial(inner_kernel, False), [in_vmem()] * 3 + [in_hbm(),...  4.22 us
    all_to_all x1, waiting for transfers between devices, per_device(): held = lax.all_to_all(slots, 'chaos', 0, 0, tiled=True)  3.63 us
    pallas_call x1, Pallas kernels, per_device(): call(pack_kernel, [in_hbm()], pltpu.HBM((32, 24, 128), f32), [pltpu.VMEM(...  2.64 us
    pallas_call x1, Pallas kernels, per_device(): call(finish_kernel, [in_vmem()] * 3, pltpu.HBM(right_side.shape, f32), [p...  1.17 us
  transfers between devices with their start and end apart: 4, of which 1 were waited for; matrix products, arithmetic and copies ran while one was open for 0% of the time, Pallas kernels for 18%

profile of v5, /device:TPU:1, one launch (start us, length us, event | category | flops | bytes accessed | tf_op | source)
XLA Modules:
  0.0 53.2 jit_solution(1185054304415738524)
XLA Ops:
  0.0 2.6 %pack_kernel.1 = f32[32,24,128]{2,1,0:T(8,128)} custom-call(f32[16,32,128]{2,1,0:T(8,128)} %source.3), custom_call_target="tpu_custom_call" | custom-call | tf_op jit(solution)/shard_map/pack_kernel/pallas_call | solution.py:509
  2.7 10.4 %all-to-all-start = ((f32[32,24,128]{2,1,0:T(8,128)}), f32[32,24,128]{2,1,0:T(8,128)S(1)}, u32[]{:S(2)}, u32[]{:S(2)}) async-start(f32[32,24,128]{2,1,0:T(8,128)} %pack_kernel.1), calls=%async_computation | async-start | bytes 786432 | tf_op jit(solution)/shard_map/all_to_all | solution.py:522
  14.4 5.4 %prepare_kernel.1 = (bf16[8,10,64,256]{3,2,1,0:T(8,128)(2,1)S(1)}, f32[48,128]{1,0:T(8,128)S(1)}, f32[16,128]{1,0:T(8,128)S(1)}) custom-call(bf16[160,4096]{1,0:T(8,128)(2,1)} %bitcast.2, s32[2,10]{1,0:T(2,128)} %bitcast.3, f32[32,128]{1,0:T(8,128)} %mean_at.1, f32[10,32,128]{2,1,0:T(8,128)} %mode_at.1, f32[1]{0:T(128)S(6)} %copy.10.lower_bound, ...), custom_call_target="tpu_custom_call" | custom-call | flops 134217728 | bytes 4194304 | tf_op jit(solution)/shard_map/prepare_kernel/pallas_call | solution.py:524
  19.7 3.6 %all-to-all-done.slots = f32[32,24,128]{2,1,0:T(8,128)S(1)} async-done(((f32[32,24,128]{2,1,0:T(8,128)}), f32[32,24,128]{2,1,0:T(8,128)S(1)}, u32[]{:S(2)}, u32[]{:S(2)}) %all-to-all-start) | async-done | bytes 393248 | tf_op jit(solution)/shard_map/all_to_all | solution.py:522
  23.4 0.2 send_columns.1.rest_0_.columns_out
  23.5 0.7 %collective-permute-start.1 = (f32[80,128]{1,0:T(8,128)S(1)}, f32[80,128]{1,0:T(8,128)S(1)}, u32[]{:S(2)}, u32[]{:S(2)}) collective-permute-start(f32[80,128]{1,0:T(8,128)S(1)} %send_columns.1.rest_0_.columns_out), channel_id=1, source_target_pairs={{192,321},{320,195},{416,257},{256,419},{432,273},{272,435},{208,3... | collective-permute-start | bytes 122888 | tf_op jit(solution)/shard_map/ppermute | solution.py:566
  24.2 0.2 send_rows.1.after.rows_out
  24.4 0.7 %collective-permute-start = (f32[80,128]{1,0:T(8,128)S(1)}, f32[80,128]{1,0:T(8,128)S(1)}, u32[]{:S(2)}, u32[]{:S(2)}) collective-permute-start(f32[80,128]{1,0:T(8,128)S(1)} %send_rows.1.after.rows_out), channel_id=1, source_target_pairs={{336,324},{320,348},{368,356},{352,380},{240,228},{224,252},{80,68... | collective-permute-start | bytes 122888 | tf_op jit(solution)/shard_map/ppermute | solution.py:578
  25.1 0.7 %collective-permute-start.2 = (f32[80,128]{1,0:T(8,128)S(1)}, f32[80,128]{1,0:T(8,128)S(1)}, u32[]{:S(2)}, u32[]{:S(2)}) collective-permute-start(f32[80,128]{1,0:T(8,128)S(1)} %send_again.1.rest_1_), channel_id=1, source_target_pairs={{196,325},{324,199},{420,261},{260,423},{436,277},{276,439},{212,3... | collective-permute-start | bytes 122888 | tf_op jit(solution)/shard_map/ppermute | solution.py:582
  25.8 0.0 collective-permute-done.1.rest_2_.columns_first
  25.8 4.2 %inner_after.1.inner = f32[32,16,128]{2,1,0:T(8,128)S(1)} custom-call(f32[32,24,128]{2,1,0:T(8,128)S(1)} %all-to-all-done.slots, f32[48,128]{1,0:T(8,128)S(1)} %get-tuple-element.10.coefs.rest_0_, bf16[8,10,64,256]{3,2,1,0:T(8,128)(2,1)S(1)} %get-tuple-element.11.weights, s32[2,10]{1,0:T(2,128)} %bitcast.5, ...), custom_call_target="tpu_custom_call", output_to_operand_aliasing={{}: (4, {})} | custom-call | flops 4294967296 | bytes 16777216 | tf_op jit(solution)/shard_map/inner_after/pallas_call | solution.py:583
  30.0 0.0 collective-permute-done.2.columns_later
  30.0 0.0 collective-permute-done.rows_in
  30.0 1.0 %edge_kernel.1 = (f32[32,16,128]{2,1,0:T(8,128)S(1)}, f32[16,32,128]{2,1,0:T(8,128)S(1)}) custom-call(f32[80,128]{1,0:T(8,128)S(1)} %send_rows.1.after.rows_out, f32[80,128]{1,0:T(8,128)S(1)} %collective-permute-done.rows_in, f32[80,128]{1,0:T(8,128)S(1)} %send_columns.1.rest_0_.columns_out, f32[80,128]{1,0:T(8,128)S(1)} %collective-permute-done.1.rest_2_.columns_first, ...), custom_call_target="tpu_custom_call" | custom-call | tf_op jit(solution)/shard_map/edge_kernel/pallas_call | solution.py:592
  31.0 21.0 %all_to_all.10.slots = f32[32,16,128]{2,1,0:T(8,128)S(1)} all-to-all(f32[32,16,128]{2,1,0:T(8,128)S(1)} %get-tuple-element.13), channel_id=1, replica_groups={{320,336,352,368,384,400,416,432,448,464,480,496,0,16,32,48,64,80,96,11..., dimensions={0} | all-to-all | bytes 524288 | tf_op jit(solution)/shard_map/all_to_all | solution.py:607
  52.0 1.2 %finish_kernel.1 = f32[16,32,128]{2,1,0:T(8,128)} custom-call(f32[16,32,128]{2,1,0:T(8,128)S(1)} %get-tuple-element.12.field, f32[32,16,128]{2,1,0:T(8,128)S(1)} %all_to_all.10.slots, f32[16,128]{1,0:T(8,128)S(1)} %get-tuple-element.14.scales), custom_call_target="tpu_custom_call" | custom-call | tf_op jit(solution)/shard_map/finish_kernel/pallas_call | solution.py:608
  (2 shorter events, 0.0 us)
Async XLA Ops:
  2.7 20.7 %all-to-all-start = ((f32[32,24,128]{2,1,0:T(8,128)}), f32[32,24,128]{2,1,0:T(8,128)S(1)}, u32[]{:S(2)}, u32[]{:S(2)}) async-start(f32[32,24,128]{2,1,0:T(8,128)} %pack_kernel.1), calls=%async_computation | async-start | bytes 786432 | tf_op jit(solution)/shard_map/all_to_all | solution.py:522
  23.5 2.2 %collective-permute-start.1 = (f32[80,128]{1,0:T(8,128)S(1)}, f32[80,128]{1,0:T(8,128)S(1)}, u32[]{:S(2)}, u32[]{:S(2)}) collective-permute-start(f32[80,128]{1,0:T(8,128)S(1)} %send_columns.1.rest_0_.columns_out), channel_id=1, source_target_pairs={{192,321},{320,195},{416,257},{256,419},{432,273},{272,435},{208,3... | collective-permute-start | bytes 122888 | tf_op jit(solution)/shard_map/ppermute | solution.py:566
  24.4 5.6 %collective-permute-start = (f32[80,128]{1,0:T(8,128)S(1)}, f32[80,128]{1,0:T(8,128)S(1)}, u32[]{:S(2)}, u32[]{:S(2)}) collective-permute-start(f32[80,128]{1,0:T(8,128)S(1)} %send_rows.1.after.rows_out), channel_id=1, source_target_pairs={{336,324},{320,348},{368,356},{352,380},{240,228},{224,252},{80,68... | collective-permute-start | bytes 122888 | tf_op jit(solution)/shard_map/ppermute | solution.py:578
  25.1 4.9 %collective-permute-start.2 = (f32[80,128]{1,0:T(8,128)S(1)}, f32[80,128]{1,0:T(8,128)S(1)}, u32[]{:S(2)}, u32[]{:S(2)}) collective-permute-start(f32[80,128]{1,0:T(8,128)S(1)} %send_again.1.rest_1_), channel_id=1, source_target_pairs={{196,325},{324,199},{420,261},{260,423},{436,277},{276,439},{212,3... | collective-permute-start | bytes 122888 | tf_op jit(solution)/shard_map/ppermute | solution.py:582
